TPU v7x, 512 devices: a whole 4x8x8 slice. The times are simulated.
512 devices in a mesh: dp: 32 (over x, y), tile: 16 (over z, core).
Axes of the slice: x: 4, y: 8, z: 8, core: 2. Of those that a mesh axis runs over, the one named last changes fastest.
Arguments:
- inputs: bfloat16 [32, 32, 512, 256], P('dp', None, 'tile'), may hold values from -6 to 6
- kernel: bfloat16 [2304, 256], replicated, may hold values from -0.125 to 0.125
- cotangent: bfloat16 [32, 32, 512, 256], P('dp', None, 'tile'), may hold values from -6 to 6
- feedback: float32 [32, 2304, 256], P('dp', 'tile'), may hold values from -4 to 4
- q_start: float32 [256, 8], replicated, may hold values from -6 to 6
Outputs:
- output: bfloat16 [32, 32, 512, 256], P('dp', None, 'tile')
- input_grad: bfloat16 [32, 32, 512, 256], P('dp', None, 'tile')
- p_factor: float32 [2304, 8], P('tile')
- q_factor: float32 [256, 8], replicated
- new_feedback: float32 [32, 2304, 256], P('dp', 'tile')
All inputs are finite; a program needn't handle non-finite values.
Results may differ from a plain program's by a relative error of at most 0.017.
Values may be sent and summed in bfloat16 or wider, within the bound.
No kernel may reach another device: no remote copies, remote signals or barrier semaphores. Data moves between devices by JAX's collectives and lax.ppermute only.
A program may use at most 64 MiB of HBM per device.

v0:
```python
import math

import jax
import jax.numpy as jnp
from jax import lax
from jax.sharding import PartitionSpec as P


def extended(block, sides, width):
    for axis, dim in sides:
        count = lax.axis_size(axis)
        forward = [(i, i + 1) for i in range(count - 1)]
        forward.append((count - 1, 0))
        backward = [(target, source) for source, target in forward]
        low = lax.ppermute(
            lax.slice_in_dim(block, block.shape[dim] - width, None, axis=dim), axis, forward
        )
        high = lax.ppermute(lax.slice_in_dim(block, 0, width, axis=dim), axis, backward)
        block = jnp.concatenate([low, block, high], axis=dim)
    return block


def tap_windows(padded, flip_sign, lat_count, lon_count):
    pieces = []
    for lat_step in (-1, 0, 1):
        for lon_step in (-1, 0, 1):
            lat_begin = 1 + flip_sign * lat_step
            lon_begin = 1 + flip_sign * lon_step
            pieces.append(
                padded[:, lat_begin : lat_begin + lat_count, lon_begin : lon_begin + lon_count, :]
            )
    return jnp.concatenate(pieces, axis=3)


def input_rimmed(image):
    rimmed = extended(image, (("tile", 2),), 1)
    return jnp.pad(rimmed, ((0, 0), (1, 1), (0, 0), (0, 0)))


def slope_rimmed(image):
    rimmed = extended(image, (("tile", 2),), 1)
    return jnp.pad(rimmed, ((0, 0), (1, 1), (0, 0), (0, 0)))


def reduce_rows(row_term, rows_dev):
    return lax.psum_scatter(
        row_term(jnp.int32(0), lax.axis_size("tile") * rows_dev).astype(jnp.bfloat16),
        "tile",
        scatter_dimension=0,
        tiled=True,
    ).astype(jnp.float32)


def orthonormal(vectors, wider):
    basis = jnp.zeros_like(vectors)
    basis_wide = jnp.zeros_like(wider)
    for column in range(vectors.shape[1]):
        vector = vectors[:, column]
        vector_wide = wider[:, column]
        projected = lax.psum(jnp.dot(basis.T, vector, precision=lax.Precision.HIGHEST), "tile")
        remain = vector - jnp.dot(basis, projected, precision=lax.Precision.HIGHEST)
        remain_wide = vector_wide - jnp.dot(basis_wide, projected, precision=lax.Precision.HIGHEST)
        sq_norm = lax.psum(jnp.sum(remain * remain), "tile")
        basis = basis.at[:, column].set(remain / jnp.sqrt(sq_norm))
        basis_wide = basis_wide.at[:, column].set(remain_wide / jnp.sqrt(sq_norm))
    return (basis, basis_wide)


def per_device(inputs, kernel, cotangent, feedback, q_start):
    lat_count = inputs.shape[1]
    lon_dev = inputs.shape[2]
    channels = inputs.shape[3]
    kernel_rows = kernel.shape[0]
    rows_dev = feedback.shape[1]
    cells = lat_count * lon_dev
    num_images = lax.axis_size("dp")
    grad_scale = 1.0 / math.sqrt(lat_count * lon_dev * lax.axis_size("tile"))
    patches = tap_windows(input_rimmed(inputs), 1, lat_count, lon_dev).reshape(cells, kernel_rows)
    preact = jnp.dot(patches, kernel, preferred_element_type=jnp.float32)
    sigmoid_vals = jax.nn.sigmoid(preact)
    output = (preact * sigmoid_vals).astype(jnp.bfloat16).reshape(1, lat_count, lon_dev, channels)
    upstream_flat = cotangent.reshape(cells, channels).astype(jnp.float32)
    slope = (upstream_flat * sigmoid_vals * (1.0 + preact * (1.0 - sigmoid_vals))).astype(
        jnp.bfloat16
    )
    slope_image = slope.reshape(1, lat_count, lon_dev, channels)
    slope_patches = tap_windows(slope_rimmed(slope_image), -1, lat_count, lon_dev).reshape(
        cells, kernel_rows
    )
    flipped = (
        kernel.reshape(9, channels, channels).transpose(0, 2, 1).reshape(kernel_rows, channels)
    )
    input_grad = jnp.dot(slope_patches, flipped, preferred_element_type=jnp.float32).astype(
        jnp.bfloat16
    )
    input_grad = input_grad.reshape(1, lat_count, lon_dev, channels)
    own_error = feedback[0]

    def row_term(begin_row, row_total):
        term = lax.dot_general(
            patches, slope, (((0,), (0,)), ((), ())), preferred_element_type=jnp.float32
        )
        return term * grad_scale

    matrix = reduce_rows(row_term, rows_dev) + own_error
    p_local = jnp.dot(matrix, q_start, precision=lax.Precision.HIGHEST)
    p_sum = lax.psum(p_local, "dp") / num_images
    p_factor, unused_wide = orthonormal(p_sum, p_sum)
    q_part = jnp.dot(matrix.T, p_factor, precision=lax.Precision.HIGHEST)
    q_factor = lax.psum(q_part, ("dp", "tile")) / num_images
    approx = jnp.dot(p_factor, q_factor.T, precision=lax.Precision.HIGHEST)
    new_feedback = (matrix - approx)[None]
    return (output, input_grad, p_factor, q_factor, new_feedback)


def solution(mesh):
    in_specs = (
        P("dp", None, "tile", None),
        P(),
        P("dp", None, "tile", None),
        P("dp", "tile", None),
        P(),
    )
    out_specs = (
        P("dp", None, "tile", None),
        P("dp", None, "tile", None),
        P("tile", None),
        P(),
        P("dp", "tile", None),
    )
    return jax.shard_map(
        per_device, mesh=mesh, in_specs=in_specs, out_specs=out_specs, check_vma=False
    )
```

profile of v0, /device:TPU:1, one launch (start us, length us, event | category | flops | bytes accessed | tf_op | source)
XLA Modules:
  0.0 678.7 jit_solution(2678761481754613671)
XLA Ops:
  7.2 1.1 fusion.46
  8.3 3.5 collective-permute-start
  11.8 3.4 collective-permute-start.1
  16.1 1.4 select_maximum_fusion.2
  19.2 2.4 fusion.4
  21.6 2.5 fusion
  24.2 3.9 collective-permute-start.3
  28.0 1.5 copy.10
  34.7 1.1 fusion.44
  37.9 47.2 %reduce-scatter.2.cloned.1.call-done = bf16[144,256]{1,0:T(8,128)(2,1)} async-done(((bf16[2304,256]{1,0:T(8,128)(2,1)}), bf16[144,256]{1,0:T(8,128)(2,1)}) %reduce-scatter.2.cloned.1.call-update) | async-done | bytes 73744 | tf_op jit(solution)/shard_map/reduce_scatter | solution.py:46
  85.2 1.1 fusion.9
  86.3 61.6 %psum.126 = f32[144,8]{0,1:T(8,128)S(1)} all-reduce(f32[144,8]{0,1:T(8,128)S(1)} %fusion.9), channel_id=1, replica_groups=mesh['dp'=32,'tile'=16] {'dp'}, use_global_device_ids=true, to_apply=%region_2.3 | all-reduce | flops 1152 | bytes 9216 | tf_op jit(solution)/shard_map/psum | solution.py:107
  148.0 1.9 constant_dynamic-update-slice_fusion.7
  149.9 40.5 %psum.127 = f32[8]{0:T(128)S(1)} all-reduce(f32[8]{0:T(128)S(1)} %convolution_bitcast_fusion.7), channel_id=1, replica_groups=mesh['dp'=32,'tile'=16] {'tile'}, use_global_device_ids=true, to_apply=%region_3.4 | all-reduce | flops 8 | bytes 64 | tf_op jit(solution)/shard_map/psum | solution.py:60
  192.3 24.2 %psum.128 = f32[]{:T(128)} all-reduce(f32[]{:T(128)} %get-tuple-element.115), channel_id=1, replica_groups=mesh['dp'=32,'tile'=16] {'tile'}, use_global_device_ids=true, to_apply=%region_5.6 | all-reduce | flops 1 | bytes 8 | tf_op jit(solution)/shard_map/psum | solution.py:63
  218.8 23.5 %psum.129 = f32[8]{0:T(128)S(1)} all-reduce(f32[8]{0:T(128)S(1)} %convolution_bitcast_fusion.6), channel_id=1, replica_groups=mesh['dp'=32,'tile'=16] {'tile'}, use_global_device_ids=true, to_apply=%region_7.8 | all-reduce | flops 8 | bytes 64 | tf_op jit(solution)/shard_map/psum | solution.py:60
  243.1 24.2 %psum.130 = f32[]{:T(128)} all-reduce(f32[]{:T(128)} %get-tuple-element.113), channel_id=1, replica_groups=mesh['dp'=32,'tile'=16] {'tile'}, use_global_device_ids=true, to_apply=%region_9.10 | all-reduce | flops 1 | bytes 8 | tf_op jit(solution)/shard_map/psum | solution.py:63
  269.6 23.5 %psum.131 = f32[8]{0:T(128)S(1)} all-reduce(f32[8]{0:T(128)S(1)} %convolution_bitcast_fusion.5), channel_id=1, replica_groups=mesh['dp'=32,'tile'=16] {'tile'}, use_global_device_ids=true, to_apply=%region_11.12 | all-reduce | flops 8 | bytes 64 | tf_op jit(solution)/shard_map/psum | solution.py:60
  293.9 24.2 %psum.132 = f32[]{:T(128)} all-reduce(f32[]{:T(128)} %get-tuple-element.111), channel_id=1, replica_groups=mesh['dp'=32,'tile'=16] {'tile'}, use_global_device_ids=true, to_apply=%region_13.14 | all-reduce | flops 1 | bytes 8 | tf_op jit(solution)/shard_map/psum | solution.py:63
  320.5 23.5 %psum.133 = f32[8]{0:T(128)S(1)} all-reduce(f32[8]{0:T(128)S(1)} %convolution_bitcast_fusion.4), channel_id=1, replica_groups=mesh['dp'=32,'tile'=16] {'tile'}, use_global_device_ids=true, to_apply=%region_15.16 | all-reduce | flops 8 | bytes 64 | tf_op jit(solution)/shard_map/psum | solution.py:60
  344.8 24.2 %psum.134 = f32[]{:T(128)} all-reduce(f32[]{:T(128)} %get-tuple-element.109), channel_id=1, replica_groups=mesh['dp'=32,'tile'=16] {'tile'}, use_global_device_ids=true, to_apply=%region_17.18 | all-reduce | flops 1 | bytes 8 | tf_op jit(solution)/shard_map/psum | solution.py:63
  371.2 23.5 %psum.135 = f32[8]{0:T(128)S(1)} all-reduce(f32[8]{0:T(128)S(1)} %convolution_bitcast_fusion.3), channel_id=1, replica_groups=mesh['dp'=32,'tile'=16] {'tile'}, use_global_device_ids=true, to_apply=%region_19.20 | all-reduce | flops 8 | bytes 64 | tf_op jit(solution)/shard_map/psum | solution.py:60
  395.5 24.2 %psum.136 = f32[]{:T(128)} all-reduce(f32[]{:T(128)} %get-tuple-element.107), channel_id=1, replica_groups=mesh['dp'=32,'tile'=16] {'tile'}, use_global_device_ids=true, to_apply=%region_21.22 | all-reduce | flops 1 | bytes 8 | tf_op jit(solution)/shard_map/psum | solution.py:63
  422.1 23.5 %psum.137 = f32[8]{0:T(128)S(1)} all-reduce(f32[8]{0:T(128)S(1)} %convolution_bitcast_fusion.2), channel_id=1, replica_groups=mesh['dp'=32,'tile'=16] {'tile'}, use_global_device_ids=true, to_apply=%region_23.24 | all-reduce | flops 8 | bytes 64 | tf_op jit(solution)/shard_map/psum | solution.py:60
  446.4 24.2 %psum.138 = f32[]{:T(128)} all-reduce(f32[]{:T(128)} %get-tuple-element.105), channel_id=1, replica_groups=mesh['dp'=32,'tile'=16] {'tile'}, use_global_device_ids=true, to_apply=%region_25.26 | all-reduce | flops 1 | bytes 8 | tf_op jit(solution)/shard_map/psum | solution.py:63
  473.0 23.5 %psum.139 = f32[8]{0:T(128)S(1)} all-reduce(f32[8]{0:T(128)S(1)} %convolution_bitcast_fusion.1), channel_id=1, replica_groups=mesh['dp'=32,'tile'=16] {'tile'}, use_global_device_ids=true, to_apply=%region_27.28 | all-reduce | flops 8 | bytes 64 | tf_op jit(solution)/shard_map/psum | solution.py:60
  497.2 24.2 %psum.140 = f32[]{:T(128)} all-reduce(f32[]{:T(128)} %get-tuple-element.103), channel_id=1, replica_groups=mesh['dp'=32,'tile'=16] {'tile'}, use_global_device_ids=true, to_apply=%region_29.30 | all-reduce | flops 1 | bytes 8 | tf_op jit(solution)/shard_map/psum | solution.py:63
  523.0 4.9 convolution_convert_fusion
  527.9 23.5 %psum.141 = f32[8]{0:T(128)S(1)} all-reduce(f32[8]{0:T(128)S(1)} %convolution_bitcast_fusion), channel_id=1, replica_groups=mesh['dp'=32,'tile'=16] {'tile'}, use_global_device_ids=true, to_apply=%region_30.31 | all-reduce | flops 8 | bytes 64 | tf_op jit(solution)/shard_map/psum | solution.py:60
  552.1 24.2 %psum.142 = f32[]{:T(128)} all-reduce(f32[]{:T(128)} %get-tuple-element.101), channel_id=1, replica_groups=mesh['dp'=32,'tile'=16] {'tile'}, use_global_device_ids=true, to_apply=%region_32.33 | all-reduce | flops 1 | bytes 8 | tf_op jit(solution)/shard_map/psum | solution.py:63
  577.2 93.6 %psum.143 = f32[256,8]{0,1:T(8,128)S(1)} all-reduce(f32[256,8]{0,1:T(8,128)S(1)} %fusion.8), channel_id=1, replica_groups=mesh['dp'=32,'tile'=16] {'dp','tile'}, use_global_device_ids=true, to_apply=%region_33.34 | all-reduce | flops 2048 | bytes 16384 | tf_op jit(solution)/shard_map/psum | solution.py:110
  670.8 1.0 fusion.2
  (100 shorter events, 28.3 us)
Async XLA Ops:
  7.2 78.0 %copy-start = (f32[256,8]{0,1:T(8,128)S(1)}, f32[256,8]{0,1:T(8,128)}, u32[]{:S(2)}) copy-start(f32[256,8]{0,1:T(8,128)} %param.25) | copy-start | bytes 24580
  7.2 10.9 %copy-start.1 = (bf16[1,32,32,256]{3,2,1,0:T(8,128)(2,1)S(1)}, bf16[1,32,32,256]{3,2,1,0:T(8,128)(2,1)}, u32[]{:S(2)}) copy-start(bf16[1,32,32,256]{3,2,1,0:T(8,128)(2,1)} %param.21) | copy-start | bytes 1572868
  7.2 78.0 %reduce-scatter.2.cloned.1.call-start = ((), (), s32[]{:S(2)}) async-start(), calls=%async_computation.1 | async-start | bytes 1253376 | tf_op jit(solution)/shard_map/reduce_scatter | solution.py:46
  8.3 7.6 %collective-permute-start = (bf16[1,32,1,256]{3,2,1,0:T(2,128)(2,1)S(1)}, bf16[1,32,1,256]{3,2,1,0:T(2,128)(2,1)S(1)}, u32[]{:S(2)}, u32[]{:S(2)}) collective-permute-start(bf16[1,32,1,256]{3,2,1,0:T(2,128)(2,1)S(1)} %get-tuple-element.129), channel_id=1, source_target_pairs={{0,1},{1,2},{2,3},{3,4},{4,5},{5,6},{6,7},{7,8},{8,9},{9,10},{10,1... | collective-permute-start | bytes 49160 | tf_op jit(solution)/shard_map/ppermute | solution.py:15
  11.8 4.3 collective-permute-start.1
  17.5 1.7 copy-start.4
  17.5 1.7 copy-start.7
  24.2 10.1 %collective-permute-start.2 = (bf16[1,32,1,256]{3,2,1,0:T(2,128)(2,1)S(1)}, bf16[1,32,1,256]{3,2,1,0:T(2,128)(2,1)S(1)}, u32[]{:S(2)}, u32[]{:S(2)}) collective-permute-start(bf16[1,32,1,256]{3,2,1,0:T(2,128)(2,1)S(1)} %get-tuple-element.127), channel_id=1, source_target_pairs={{0,1},{1,2},{2,3},{3,4},{4,5},{5,6},{6,7},{7,8},{8,9},{9,10},{10,1... | collective-permute-start | bytes 49160 | tf_op jit(solution)/shard_map/ppermute | solution.py:15
  24.2 10.1 %collective-permute-start.3 = (bf16[1,32,1,256]{3,2,1,0:T(2,128)(2,1)S(1)}, bf16[1,32,1,256]{3,2,1,0:T(2,128)(2,1)S(1)}, u32[]{:S(2)}, u32[]{:S(2)}) collective-permute-start(bf16[1,32,1,256]{3,2,1,0:T(2,128)(2,1)S(1)} %get-tuple-element.128), channel_id=1, source_target_pairs={{1,0},{2,1},{3,2},{4,3},{5,4},{6,5},{7,6},{8,7},{9,8},{10,9},{11,1... | collective-permute-start | bytes 49160 | tf_op jit(solution)/shard_map/ppermute | solution.py:18
  34.7 50.5 %copy-start.3 = (f32[1,144,256]{2,1,0:T(8,128)S(1)}, f32[1,144,256]{2,1,0:T(8,128)}, u32[]{:S(2)}) copy-start(f32[1,144,256]{2,1,0:T(8,128)} %param.24) | copy-start | bytes 442372
  523.0 54.1 %copy-start.5 = (bf16[144,256]{1,0:T(8,128)(2,1)S(1)}, bf16[144,256]{1,0:T(8,128)(2,1)}, u32[]{:S(2)}) copy-start(bf16[144,256]{1,0:T(8,128)(2,1)} %reduce-scatter.2.cloned.1.call-done) | copy-start | bytes 221188
  577.0 94.8 %copy-start.2 = (f32[144,8]{0,1:T(8,128)}, f32[144,8]{0,1:T(8,128)S(1)}, u32[]{:S(2)}) copy-start(f32[144,8]{0,1:T(8,128)S(1)} %scatter.39) | copy-start | bytes 13828
  670.8 1.0 copy-start.6
Sparse Core Ops, SparseCore 0:
  24.2 60.9 reduce-scatter.1
where the time goes:
time: 679 us
  blocking collectives  554 us (82%)
  waiting for transfers between devices  48.1 us (7%)
  between operations  19.9 us (3%)
  other arithmetic  17.6 us (3%)
  local copies, waits for them, and re-layouts  14.7 us (2%)
  matrix products  14 us (2%)
  starting transfers between devices  10.8 us (2%)
    psum x8, blocking collectives, orthonormal(): lax.psum(jnp.dot(basis.T, vector, precision=lax.Precision.HIGHEST), 'tile')  205 us
    psum x8, blocking collectives, orthonormal(): sq_norm = lax.psum(jnp.sum(remain * remain), 'tile')  193 us
    psum x1, blocking collectives, per_device(): q_factor = lax.psum(q_part, ('dp', 'tile')) / num_images  93.6 us
    psum x1, blocking collectives, per_device(): p_sum = lax.psum(p_local, 'dp') / num_images  61.6 us
    reduce_scatter x1, waiting for transfers between devices, reduce_rows(): lax.psum_scatter(row_term(jnp.int32(0), lax.axis_size('tile') * rows_dev)...  47.2 us
  transfers between devices with their start and end apart: 5, of which 3 were waited for; matrix products, arithmetic and copies ran while one was open for 1% of the time, Pallas kernels for 0%

commit v1 on v0

v1 whole, which is shorter than its diff:
```python
import functools
import math

import jax
import jax.numpy as jnp
from jax import lax
from jax.experimental import pallas as pl
from jax.experimental.pallas import tpu as pltpu
from jax.sharding import PartitionSpec as P

F32 = jnp.float32
BF16 = jnp.bfloat16
NN = (((1,), (0,)), ((), ()))
NT = (((1,), (1,)), ((), ()))
TN = (((0,), (0,)), ((), ()))
VMEM = pl.BlockSpec(memory_space=pltpu.VMEM)
SMEM = pl.BlockSpec(memory_space=pltpu.SMEM)


def dot(left, right, dims=NN):
    return lax.dot_general(left, right, dims, preferred_element_type=F32)


def in_parts(value):
    parts = []
    for _ in range(3):
        part = value.astype(BF16)
        parts.append(part)
        value = value - part.astype(F32)
    return parts


def stacked_parts(value):
    return jnp.concatenate([part.astype(F32) for part in in_parts(value)], 0).astype(BF16)


def fold(product, rank):
    return product[0:rank] + product[rank : 2 * rank] + product[2 * rank : 3 * rank]


def swish(preact, upstream):
    s = jax.nn.sigmoid(preact)
    return preact * s, upstream * s * (1.0 + preact * (1.0 - s))


def widen(source, left, right, wide, lat, lon, low, high):
    ch = source.shape[1]
    rows = 8 * lon
    column = lax.broadcasted_iota(jnp.int32, (rows, ch), 0) & (lon - 1)
    for step in range(lat // 8):
        value = source[step * rows : (step + 1) * rows, :]
        wider = value.astype(F32)
        edges = [
            jnp.broadcast_to(edge[step * 8 : step * 8 + 8, None, :], (8, lon, ch)).reshape(rows, ch)
            for edge in (left, right)
        ]
        west = jnp.where(column == 0, edges[0], pltpu.roll(wider, 1, 0))
        east = jnp.where(column == lon - 1, edges[1], pltpu.roll(wider, rows - 1, 0))
        at = slice(lon + step * rows, lon + (step + 1) * rows)
        wide[at, low * ch : (low + 1) * ch] = west.astype(BF16)
        wide[at, ch : 2 * ch] = value
        wide[at, high * ch : (high + 1) * ch] = east.astype(BF16)


def conv_kernel(
    lat, lon, tiles, scale, x_ref, cot_ref, w_ref, east_ref, west_ref, left_ref, right_ref, q_ref,
    out_ref, xgrad_ref, wgrad_ref, p_ref, x_wide, s_wide, slope_ref,
):
    cells, ch = x_ref.shape
    rank = q_ref.shape[0]
    chunk = cells // 2
    for wide in (x_wide, s_wide):
        wide[0:lon, :] = jnp.zeros((lon, 3 * ch), BF16)
        wide[lon + cells : 2 * lon + cells, :] = jnp.zeros((lon, 3 * ch), BF16)

    widen(x_ref, left_ref[1].astype(F32), right_ref[0].astype(F32), x_wide, lat, lon, 0, 2)

    def forward(step, carry):
        at = pl.multiple_of(step * chunk, chunk)
        total = dot(x_wide[pl.ds(at, chunk), :], w_ref[0 : 3 * ch, :])
        total += dot(x_wide[pl.ds(at + lon, chunk), :], w_ref[3 * ch : 6 * ch, :])
        total += dot(x_wide[pl.ds(at + 2 * lon, chunk), :], w_ref[6 * ch : 9 * ch, :])
        out, slope = swish(total, cot_ref[pl.ds(at, chunk), :].astype(F32))
        out_ref[pl.ds(at, chunk), :] = out.astype(BF16)
        slope_ref[pl.ds(at, chunk), :] = slope.astype(BF16)
        return carry

    lax.fori_loop(0, cells // chunk, forward, 0)

    columns = [
        jnp.concatenate([west.astype(F32), east.astype(F32)], 0)
        for west, east in (
            (left_ref[0], east_ref[1]),
            (left_ref[1], right_ref[0]),
            (west_ref[0], right_ref[1]),
        )
    ]
    row = lax.broadcasted_iota(jnp.int32, (2 * lat, ch), 0) & (lat - 1)
    total = jnp.zeros((2 * lat, ch), F32)
    for a in range(3):
        for b in range(3):
            value = columns[b]
            if a == 0:
                value = jnp.where(row == 0, 0.0, pltpu.roll(value, 1, 0))
            if a == 2:
                value = jnp.where(row == lat - 1, 0.0, pltpu.roll(value, 2 * lat - 1, 0))
            tap = 3 * a + b
            total += dot(value.astype(BF16), w_ref[tap * ch : (tap + 1) * ch, :])
    upstream = jnp.concatenate([left_ref[2].astype(F32), right_ref[2].astype(F32)], 0)
    edge = swish(total, upstream)[1].astype(BF16).astype(F32)
    widen(slope_ref, edge[:lat], edge[lat:], s_wide, lat, lon, 2, 0)

    def input_grad(step, carry):
        at = pl.multiple_of(step * chunk, chunk)
        total = None
        for a in range(3):
            for b in range(3):
                tap = 3 * a + b
                term = dot(
                    s_wide[pl.ds(at + (2 - a) * lon, chunk), b * ch : (b + 1) * ch],
                    w_ref[tap * ch : (tap + 1) * ch, :],
                    NT,
                )
                total = term if total is None else total + term
        xgrad_ref[pl.ds(at, chunk), :] = total.astype(BF16)
        return carry

    lax.fori_loop(0, cells // chunk, input_grad, 0)

    def weight_grad(a, carry):
        at = pl.multiple_of(a * lon, lon)
        for b in range(3):
            term = dot(x_wide[pl.ds(at, cells), b * ch : (b + 1) * ch], slope_ref[...], TN) * scale
            wgrad_ref[pl.ds(pl.multiple_of((3 * a + b) * ch, ch), ch), :] = term.astype(BF16)
        return carry

    lax.fori_loop(0, 3, weight_grad, 0)

    q_parts = stacked_parts(q_ref[...])
    rows = wgrad_ref.shape[0] // tiles
    for t in range(tiles):
        p_ref[t] = fold(dot(q_parts, wgrad_ref[rows * t : rows * (t + 1), :], NT), rank)


def factor_kernel(tiles, tile_ref, p_ref, wgrad_ref, error_ref, rows_ref, q_ref, flat, cut):
    rank, rows = p_ref.shape[1:]
    for t in range(tiles):
        flat[:, rows * t : rows * (t + 1)] = p_ref[t]
    vectors = flat[...]
    lane = lax.broadcasted_iota(jnp.int32, vectors.shape, 0)
    basis = jnp.zeros_like(vectors)
    for column in range(rank):
        vector = vectors[column : column + 1, :]
        remain = vector
        if column:
            projected = jnp.sum(basis * vector, axis=1, keepdims=True)
            remain = vector - jnp.sum(basis * projected, axis=0, keepdims=True)
        sq_norm = jnp.sum(remain * remain, axis=1, keepdims=True)
        basis = jnp.where(lane == column, remain / jnp.sqrt(sq_norm), basis)
    for t in range(tiles):
        cut[t] = basis[:, rows * t : rows * (t + 1)]
    own = cut[tile_ref[0]]
    rows_ref[...] = own
    total = fold(dot(stacked_parts(basis), wgrad_ref[...]), rank)
    own_parts = stacked_parts(own)
    for part in in_parts(error_ref[...]):
        total += fold(dot(own_parts, part), rank)
    q_ref[...] = total


def feedback_kernel(shares, matrix_ref, error_ref, rows_ref, q_ref, next_ref, factor_ref, left_ref):
    rank = rows_ref.shape[0]
    q_mean = q_ref[0]
    for image in range(1, shares):
        q_mean += q_ref[image]
    q_mean = q_mean * (1.0 / shares)
    factor_ref[...] = q_mean.T
    own = rows_ref[...].T
    left_ref[...] = own
    total = matrix_ref[...].astype(F32) + error_ref[...]
    for k in range(rank):
        total -= own[:, k : k + 1] * q_mean[k : k + 1, :]
    next_ref[...] = total


def shift(axis, step):
    count = lax.axis_size(axis)
    return [(i, (i + step) % count) for i in range(count)]


def shares_of(value, axis):
    count = lax.axis_size(axis)
    return lax.all_to_all(
        jnp.broadcast_to(value[None], (count,) + value.shape), axis, 0, 0, tiled=True
    )


def per_device(inputs, kernel, cotangent, feedback, q_start):
    _, lat, lon, ch = inputs.shape
    kernel_rows = kernel.shape[0]
    rows_dev = feedback.shape[1]
    rank = q_start.shape[1]
    cells = lat * lon
    tiles = lax.axis_size("tile")
    images = lax.axis_size("dp")
    scale = 1.0 / math.sqrt(cells * tiles)
    x, upstream, error = inputs[0], cotangent[0], feedback[0]

    def edge(*columns):
        return jnp.stack(columns)

    east = edge(x[:, lon - 2], x[:, lon - 1], upstream[:, lon - 1])
    west = edge(x[:, 0], x[:, 1], upstream[:, 0])
    left = lax.ppermute(east, "tile", shift("tile", 1))
    right = lax.ppermute(west, "tile", shift("tile", -1))

    q_rows = q_start.T
    sds = jax.ShapeDtypeStruct
    out, xgrad, wgrad, p_shares = pl.pallas_call(
        functools.partial(conv_kernel, lat, lon, tiles, scale),
        out_shape=(
            sds((cells, ch), BF16),
            sds((cells, ch), BF16),
            sds((kernel_rows, ch), BF16),
            sds((tiles, rank, rows_dev), F32),
        ),
        in_specs=[VMEM] * 8,
        out_specs=(VMEM,) * 4,
        scratch_shapes=[
            pltpu.VMEM((cells + 2 * lon, 3 * ch), BF16),
            pltpu.VMEM((cells + 2 * lon, 3 * ch), BF16),
            pltpu.VMEM((cells, ch), BF16),
        ],
        compiler_params=pltpu.CompilerParams(vmem_limit_bytes=40 * 2**20),
        name="conv",
    )(x.reshape(cells, ch), upstream.reshape(cells, ch), kernel, east, west, left, right, q_rows)

    matrix = lax.psum_scatter(wgrad, "tile", scatter_dimension=0, tiled=True)

    error_rows = lax.dot_general(q_rows, error, NT, precision=lax.Precision.HIGHEST)
    p_local = lax.all_to_all(p_shares, "tile", 0, 0, tiled=True).sum(0) + error_rows
    p_rows = shares_of(p_local, "dp").sum(0) * (1.0 / images)
    p_all = shares_of(p_rows, "tile")

    tile = lax.axis_index("tile").astype(jnp.int32)[None]
    own_rows, q_part = pl.pallas_call(
        functools.partial(factor_kernel, tiles),
        out_shape=(sds((rank, rows_dev), F32), sds((rank, ch), F32)),
        in_specs=[SMEM] + [VMEM] * 3,
        out_specs=(VMEM,) * 2,
        scratch_shapes=[
            pltpu.VMEM((rank, kernel_rows), F32),
            pltpu.VMEM((tiles, rank, rows_dev), F32),
        ],
        compiler_params=pltpu.CompilerParams(vmem_limit_bytes=16 * 2**20),
        name="factor",
    )(tile, p_all, wgrad, error)

    q_shares = shares_of(shares_of(q_part, "tile").sum(0), "dp")
    new_feedback, q_factor, p_factor = pl.pallas_call(
        functools.partial(feedback_kernel, images),
        out_shape=(sds((rows_dev, ch), F32), sds((ch, rank), F32), sds((rows_dev, rank), F32)),
        in_specs=[VMEM] * 4,
        out_specs=(VMEM,) * 3,
        compiler_params=pltpu.CompilerParams(vmem_limit_bytes=16 * 2**20),
        name="residual",
    )(matrix, error, own_rows, q_shares)

    shape = inputs.shape
    return (out.reshape(shape), xgrad.reshape(shape), p_factor, q_factor, new_feedback[None])


def solution(mesh):
    in_specs = (
        P("dp", None, "tile", None),
        P(),
        P("dp", None, "tile", None),
        P("dp", "tile", None),
        P(),
    )
    out_specs = (
        P("dp", None, "tile", None),
        P("dp", None, "tile", None),
        P("tile", None),
        P(),
        P("dp", "tile", None),
    )
    return jax.shard_map(
        per_device, mesh=mesh, in_specs=in_specs, out_specs=out_specs, check_vma=False
    )
```

time: 679 us -> 121 us (0.18)
  blocking collectives: 554 us -> 63.8 us
  waiting for transfers between devices: 48.1 us -> 12.4 us
  other arithmetic: 17.6 us -> 0.1 us
  matrix products: 14 us -> 0.18 us
  Pallas kernels: 0 us -> 11.6 us
  local copies, waits for them, and re-layouts: 14.7 us -> 4.79 us
    psum x18 -> x0, blocking collectives: 554 us -> none  [the longest x8 205 us: orthonormal(): lax.psum(jnp.dot(basis.T, vector, precision=lax.Precision.HIGHEST), 'tile')]
    all_to_all x0 -> x4, blocking collectives: none -> 63.8 us  [the longest x3 48.1 us: shares_of(): lax.all_to_all(jnp.broadcast_to(value[None], (count,) + value.shape), axi...]
    reduce_scatter x1, waiting for transfers between devices: 47.2 us -> 0.01 us  [per_device(): matrix = lax.psum_scatter(wgrad, 'tile', scatter_dimension=0, tiled=True)]
    dot_general x21 -> x1, matrix products: 14 us -> 0.18 us  [per_device(): lax.dot_general(q_rows, error, NT, precision=lax.Precision.HIGHEST)]
    pallas_call x0 -> x3, Pallas kernels: none -> 11.6 us  [the longest x1 7.31 us: per_device(): pl.pallas_call(functools.partial(conv_kernel, lat, lon, tiles, scale), ou...]
    another operation x14 -> x2, other arithmetic: 9.2 us -> 0.02 us  [edge(): return jnp.stack(columns)]
    all_to_all x0 -> x1, waiting for transfers between devices: none -> 8.58 us  [shares_of(): lax.all_to_all(jnp.broadcast_to(value[None], (count,) + value.shape), axi...]
  transfers between devices with their start and end apart: 5 -> 4, of which waited for: 3 -> 3; matrix products, arithmetic and copies ran while one was open for 1% -> 1% of each run, Pallas kernels for 0% -> 3%
where the time goes in v1:
time: 121 us; the launch traced here: 119 us
  blocking collectives  63.8 us (53%)
  between operations  14.2 us (12%)
  waiting for transfers between devices  12.4 us (10%)
  starting transfers between devices  11.9 us (10%)
  Pallas kernels  11.6 us (10%)
  local copies, waits for them, and re-layouts  4.79 us (4%)
    all_to_all x3, blocking collectives, shares_of(): lax.all_to_all(jnp.broadcast_to(value[None], (count,) + value.shape), axi...  48.1 us
    all_to_all x1, blocking collectives, per_device(): lax.all_to_all(p_shares, 'tile', 0, 0, tiled=True).sum(0) + error_rows  15.7 us
    all_to_all x1, waiting for transfers between devices, shares_of(): lax.all_to_all(jnp.broadcast_to(value[None], (count,) + value.shape), axi...  8.58 us
    pallas_call x1, Pallas kernels, per_device(): pl.pallas_call(functools.partial(conv_kernel, lat, lon, tiles, scale), ou...  7.31 us
    ppermute x1, starting transfers between devices, per_device(): right = lax.ppermute(west, 'tile', shift('tile', -1))  6.89 us
    all_to_all x1, starting transfers between devices, shares_of(): lax.all_to_all(jnp.broadcast_to(value[None], (count,) + value.shape), axi...  4.99 us
    unnamed x16, local copies, waits for them, and re-layouts  4.01 us
    pallas_call x1, Pallas kernels, per_device(): pl.pallas_call(functools.partial(factor_kernel, tiles), out_shape=(sds((r...  3.32 us
  transfers between devices with their start and end apart: 4, of which 3 were waited for; matrix products, arithmetic and copies ran while one was open for 1% of the time, Pallas kernels for 3%

profile of v1, /device:TPU:1, one launch (start us, length us, event | category | flops | bytes accessed | tf_op | source)
XLA Modules:
  0.0 119.1 jit_solution(7536402081214305938)
XLA Ops:
  7.2 0.0 copy-start.1
  7.2 0.0 copy-start
  7.2 0.0 copy-start.5
  7.2 0.0 copy-start.3
  7.2 0.0 reduce-scatter.2.cloned.1.call-start
  7.3 1.5 %copy.20 = bf16[1,32,32,256]{3,1,2,0:T(8,128)(2,1)S(1)} copy(bf16[1,32,32,256]{3,2,1,0:T(8,128)(2,1)} %param.7) | data formatting | bytes 1048576 | tf_op args[2]
  8.7 0.0 copy-done
  8.7 0.3 copy.21
  9.1 6.9 %collective-permute-start.1 = (bf16[3,32,256]{2,1,0:T(8,128)(2,1)S(1)}, bf16[3,32,256]{2,1,0:T(8,128)(2,1)S(1)}, u32[]{:S(2)}, u32[]{:S(2)}) collective-permute-start(bf16[3,32,256]{2,1,0:T(8,128)(2,1)S(1)} %pad_maximum_fusion.1.west_ref), channel_id=1, source_target_pairs={{0,15},{1,0},{2,1},{3,2},{4,3},{5,4},{6,5},{7,6},{8,7},{9,8},{10,9... | collective-permute-start | bytes 147464 | tf_op jit(solution)/shard_map/ppermute | solution.py:215
  16.0 0.0 collective-permute-start
  16.0 0.8 collective-permute-done.1.right_ref
  16.8 3.0 %collective-permute-done.left_ref = bf16[3,32,256]{2,1,0:T(8,128)(2,1)S(1)} collective-permute-done((bf16[3,32,256]{2,1,0:T(8,128)(2,1)S(1)}, bf16[3,32,256]{2,1,0:T(8,128)(2,1)S(1)}, u32[]{:S(2)}, u32[]{:S(2)}) %collective-permute-start) | collective-permute-done | bytes 49184 | tf_op jit(solution)/shard_map/ppermute | solution.py:214
  19.8 0.0 copy-done.1
  19.8 0.0 copy-done.5
  19.8 0.0 copy-done.3
  19.8 7.3 %conv.1 = (bf16[1024,256]{1,0:T(8,128)(2,1)}, bf16[1024,256]{1,0:T(8,128)(2,1)}, bf16[2304,256]{1,0:T(8,128)(2,1)}, f32[16,8,144]{2,1,0:T(8,128)S(1)}) custom-call(bf16[1024,256]{1,0:T(8,128)(2,1)S(1)} %bitcast.29, bf16[1024,256]{1,0:T(8,128)(2,1)S(1)} %bitcast.30, bf16[2304,256]{1,0:T(8,128)(2,1)S(1)} %copy-done.3, ...), custom_call_target="tpu_custom_call" | custom-call | tf_op jit(solution)/shard_map/conv/pallas_call | solution.py:219
  27.1 0.0 reduce-scatter.2.cloned.1.call-update
  27.2 15.7 %all_to_all.25 = f32[16,8,144]{2,1,0:T(8,128)S(1)} all-to-all(f32[16,8,144]{2,1,0:T(8,128)S(1)} %get-tuple-element.17), channel_id=1, replica_groups=mesh['dp'=32,'tile'=16] {'tile'}, dimensions={0} | all-to-all | bytes 147456 | tf_op jit(solution)/shard_map/all_to_all | solution.py:241
  42.9 0.0 copy-done.2
  42.9 0.2 convolution_add_fusion
  43.1 0.1 broadcast_in_dim.13
  43.2 20.2 %all_to_all.26 = f32[32,8,144]{2,1,0:T(8,128)S(1)} all-to-all(f32[32,8,144]{2,1,0:T(8,128)S(1)} %broadcast_in_dim.13), channel_id=1, replica_groups=mesh['dp'=32,'tile'=16] {'dp'}, dimensions={0} | all-to-all | bytes 294912 | tf_op jit(solution)/shard_map/all_to_all | solution.py:193
  63.5 0.7 broadcast_in_dim.14
  64.1 5.0 %all-to-all-start.2 = ((f32[16,8,144]{2,1,0:T(8,128)}), f32[16,8,144]{2,1,0:T(8,128)S(1)}, u32[]{:S(2)}, u32[]{:S(2)}) async-start(f32[16,8,144]{2,1,0:T(8,128)} %broadcast_in_dim.14), calls=%async_computation.3 | async-start | bytes 262144 | tf_op jit(solution)/shard_map/all_to_all | solution.py:193
  69.1 8.6 %all-to-all-done.2.p_ref = f32[16,8,144]{2,1,0:T(8,128)S(1)} async-done(((f32[16,8,144]{2,1,0:T(8,128)}), f32[16,8,144]{2,1,0:T(8,128)S(1)}, u32[]{:S(2)}, u32[]{:S(2)}) %all-to-all-start.2) | async-done | bytes 73760 | tf_op jit(solution)/shard_map/all_to_all | solution.py:193
  77.7 3.3 %factor.1 = (f32[8,144]{1,0:T(8,128)S(1)}, f32[8,256]{1,0:T(8,128)S(1)}) custom-call(s32[1]{0:T(128)} %bitcast.14.tile_ref, f32[16,8,144]{2,1,0:T(8,128)S(1)} %all-to-all-done.2.p_ref, bf16[2304,256]{1,0:T(8,128)(2,1)} %get-tuple-element.16.wgrad_ref, f32[144,256]{1,0:T(8,128)S(1)} %bitcast.31), custom_call_target="tpu_custom_call" | custom-call | tf_op jit(solution)/shard_map/factor/pallas_call | solution.py:246
  81.0 12.8 %all_to_all.27 = f32[16,8,256]{2,1,0:T(8,128)S(1)} all-to-all(f32[16,8,256]{2,1,0:T(8,128)S(1)} %broadcast_in_dim.15), channel_id=1, replica_groups=mesh['dp'=32,'tile'=16] {'tile'}, dimensions={0} | all-to-all | bytes 262144 | tf_op jit(solution)/shard_map/all_to_all | solution.py:193
  93.9 15.1 %all_to_all.28.q_ref = f32[32,8,256]{2,1,0:T(8,128)S(1)} all-to-all(f32[32,8,256]{2,1,0:T(8,128)S(1)} %broadcast_in_dim.16), channel_id=1, replica_groups=mesh['dp'=32,'tile'=16] {'dp'}, dimensions={0} | all-to-all | bytes 524288 | tf_op jit(solution)/shard_map/all_to_all | solution.py:193
  109.0 0.9 copy-done.4
  109.9 1.0 residual.1
  110.9 0.7 copy.16
  111.5 0.7 copy.17
  (12 shorter events, 0.1 us)
Async XLA Ops:
  7.2 12.7 %copy-start.1 = (bf16[1,32,32,256]{3,2,1,0:T(8,128)(2,1)S(1)}, bf16[1,32,32,256]{3,2,1,0:T(8,128)(2,1)}, u32[]{:S(2)}) copy-start(bf16[1,32,32,256]{3,2,1,0:T(8,128)(2,1)} %param.7) | copy-start | bytes 1572868
  7.2 1.6 %copy-start = (bf16[1,32,32,256]{3,2,1,0:T(8,128)(2,1)S(1)}, bf16[1,32,32,256]{3,2,1,0:T(8,128)(2,1)}, u32[]{:S(2)}) copy-start(bf16[1,32,32,256]{3,2,1,0:T(8,128)(2,1)} %param.5) | copy-start | bytes 1572868
  7.2 12.6 %copy-start.5 = (f32[256,8]{0,1:T(8,128)S(1)}, f32[256,8]{0,1:T(8,128)}, u32[]{:S(2)}) copy-start(f32[256,8]{0,1:T(8,128)} %param.9) | copy-start | bytes 24580
  7.2 12.6 %copy-start.3 = (bf16[2304,256]{1,0:T(8,128)(2,1)S(1)}, bf16[2304,256]{1,0:T(8,128)(2,1)}, u32[]{:S(2)}) copy-start(bf16[2304,256]{1,0:T(8,128)(2,1)} %w_ref.1) | copy-start | bytes 3538948
  7.2 101.8 %reduce-scatter.2.cloned.1.call-start = ((), (), s32[]{:S(2)}) async-start(), calls=%async_computation.6 | async-start | bytes 1253376 | tf_op jit(solution)/shard_map/reduce_scatter | solution.py:238
  9.1 7.8 %collective-permute-start.1 = (bf16[3,32,256]{2,1,0:T(8,128)(2,1)S(1)}, bf16[3,32,256]{2,1,0:T(8,128)(2,1)S(1)}, u32[]{:S(2)}, u32[]{:S(2)}) collective-permute-start(bf16[3,32,256]{2,1,0:T(8,128)(2,1)S(1)} %pad_maximum_fusion.1.west_ref), channel_id=1, source_target_pairs={{0,15},{1,0},{2,1},{3,2},{4,3},{5,4},{6,5},{7,6},{8,7},{9,8},{10,9... | collective-permute-start | bytes 147464 | tf_op jit(solution)/shard_map/ppermute | solution.py:215
  16.0 3.8 %collective-permute-start = (bf16[3,32,256]{2,1,0:T(8,128)(2,1)S(1)}, bf16[3,32,256]{2,1,0:T(8,128)(2,1)S(1)}, u32[]{:S(2)}, u32[]{:S(2)}) collective-permute-start(bf16[3,32,256]{2,1,0:T(8,128)(2,1)S(1)} %pad_maximum_fusion.east_ref), channel_id=1, source_target_pairs={{0,1},{1,2},{2,3},{3,4},{4,5},{5,6},{6,7},{7,8},{8,9},{9,10},{10,1... | collective-permute-start | bytes 147464 | tf_op jit(solution)/shard_map/ppermute | solution.py:214
  27.1 15.8 %copy-start.2 = (f32[1,144,256]{2,1,0:T(8,128)S(1)}, f32[1,144,256]{2,1,0:T(8,128)}, u32[]{:S(2)}) copy-start(f32[1,144,256]{2,1,0:T(8,128)} %param.8) | copy-start | bytes 442372
  64.1 13.6 %all-to-all-start.2 = ((f32[16,8,144]{2,1,0:T(8,128)}), f32[16,8,144]{2,1,0:T(8,128)S(1)}, u32[]{:S(2)}, u32[]{:S(2)}) async-start(f32[16,8,144]{2,1,0:T(8,128)} %broadcast_in_dim.14), calls=%async_computation.3 | async-start | bytes 262144 | tf_op jit(solution)/shard_map/all_to_all | solution.py:193
  109.0 0.9 copy-start.4
Sparse Core Ops, SparseCore 0:
  27.3 59.1 reduce-scatter.1

commit v2 on v1

v2 whole, which is shorter than its diff:
```python
import functools
import math

import jax
import jax.numpy as jnp
from jax import lax
from jax.experimental import pallas as pl
from jax.experimental.pallas import tpu as pltpu
from jax.sharding import PartitionSpec as P

F32 = jnp.float32
BF16 = jnp.bfloat16
NN = (((1,), (0,)), ((), ()))
NT = (((1,), (1,)), ((), ()))
TN = (((0,), (0,)), ((), ()))
VMEM = pl.BlockSpec(memory_space=pltpu.VMEM)
HBM = pl.BlockSpec(memory_space=pl.ANY)
BIG = 24 * 2**20
WHOLE = 56 * 2**20


def dot(left, right, dims=NN):
    return lax.dot_general(left, right, dims, preferred_element_type=F32)


def in_parts(value):
    parts = []
    for _ in range(3):
        part = value.astype(BF16)
        parts.append(part)
        value = value - part.astype(F32)
    return parts


def stacked_parts(value):
    return jnp.concatenate([part.astype(F32) for part in in_parts(value)], 0).astype(BF16)


def fold(product, rank):
    return product[0:rank] + product[rank : 2 * rank] + product[2 * rank : 3 * rank]


def fetch(pairs, sems):
    copies = [pltpu.make_async_copy(held, place, sems.at[k]) for k, (held, place) in enumerate(pairs)]
    for copy in copies:
        copy.start()
    return copies


def swish(preact, upstream):
    s = jax.nn.sigmoid(preact)
    return preact * s, upstream * s * (1.0 + preact * (1.0 - s))


def widen(source, left, right, wide, lat, lon, low, high):
    ch = source.shape[1]
    rows = 8 * lon
    column = lax.broadcasted_iota(jnp.int32, (rows, ch), 0) & (lon - 1)
    wide[0:lon, :] = jnp.zeros((lon, 3 * ch), BF16)
    wide[lon + lat * lon :, :] = jnp.zeros((lon, 3 * ch), BF16)
    for step in range(lat // 8):
        value = source[step * rows : (step + 1) * rows, :]
        wider = value.astype(F32)
        edges = [spread(edge, step, lon) for edge in (left, right)]
        west = jnp.where(column == 0, edges[0], pltpu.roll(wider, 1, 0))
        east = jnp.where(column == lon - 1, edges[1], pltpu.roll(wider, rows - 1, 0))
        at = slice(lon + step * rows, lon + (step + 1) * rows)
        wide[at, low * ch : (low + 1) * ch] = west.astype(BF16)
        wide[at, ch : 2 * ch] = value
        wide[at, high * ch : (high + 1) * ch] = east.astype(BF16)


def spread(edge, step, lon):
    if edge is None:
        return 0.0
    ch = edge.shape[1]
    part = edge[step * 8 : step * 8 + 8, None, :]
    return jnp.broadcast_to(part, (8, lon, ch)).reshape(8 * lon, ch)


def picked(columns, source, lat, lon):
    shape = (lat * len(columns), lat * lon)
    cell = lax.broadcasted_iota(jnp.int32, shape, 1)
    row = lax.broadcasted_iota(jnp.int32, shape, 0)
    target = (row & (lat - 1)) * lon
    for k, column in enumerate(columns):
        target = jnp.where((row >= k * lat) & (row < (k + 1) * lat), target + column, target)
    return dot((cell == target).astype(F32).astype(BF16), source[...]).astype(BF16)


def load_kernel(
    lat, lon, x_hbm, cot_hbm, w_hbm, x_ref, cot_ref, w_ref, east_ref, west_ref, sems
):
    x_copy, cot_copy, w_copy = fetch([(x_hbm, x_ref), (cot_hbm, cot_ref), (w_hbm, w_ref)], sems)
    x_copy.wait()
    x_edge = picked((0, 1, lon - 2, lon - 1), x_ref, lat, lon)
    west_ref[0] = x_edge[0:lat]
    west_ref[1] = x_edge[lat : 2 * lat]
    east_ref[0] = x_edge[2 * lat : 3 * lat]
    east_ref[1] = x_edge[3 * lat : 4 * lat]
    cot_copy.wait()
    cot_edge = picked((0, lon - 1), cot_ref, lat, lon)
    west_ref[2] = cot_edge[0:lat]
    east_ref[2] = cot_edge[lat : 2 * lat]
    w_copy.wait()


def inner_kernel(lat, lon, x_ref, w_ref, x_wide, preact_ref):
    cells, ch = x_ref.shape
    chunk = cells // 2
    widen(x_ref, None, None, x_wide, lat, lon, 0, 2)

    def forward(step, carry):
        at = pl.multiple_of(step * chunk, chunk)
        total = dot(x_wide[pl.ds(at, chunk), :], w_ref[0 : 3 * ch, :])
        total += dot(x_wide[pl.ds(at + lon, chunk), :], w_ref[3 * ch : 6 * ch, :])
        total += dot(x_wide[pl.ds(at + 2 * lon, chunk), :], w_ref[6 * ch : 9 * ch, :])
        preact_ref[pl.ds(at, chunk), :] = total
        return carry

    lax.fori_loop(0, cells // chunk, forward, 0)


def conv_kernel(
    lat, lon, scale, x_wide, preact_ref, cot_ref, w_ref, east_ref, west_ref, left_ref, right_ref,
    out_hbm, slope_ref, edge_ref, keep_ref, send_ref, out_ref, wgrad_ref, out_sem,
):
    cells, ch = cot_ref.shape
    core = lax.axis_index("tile") & 1
    tap = lambda k: w_ref[k * ch : (k + 1) * ch, :]

    columns = [
        jnp.concatenate([west.astype(F32), east.astype(F32)], 0)
        for west, east in (
            (left_ref[0], east_ref[1]),
            (left_ref[1], right_ref[0]),
            (west_ref[0], right_ref[1]),
        )
    ]
    row = lax.broadcasted_iota(jnp.int32, (2 * lat, ch), 0) & (lat - 1)

    def at_latitude(value, a):
        if a == 0:
            value = jnp.where(row == 0, 0.0, pltpu.roll(value, 1, 0))
        if a == 2:
            value = jnp.where(row == lat - 1, 0.0, pltpu.roll(value, 2 * lat - 1, 0))
        return value.astype(BF16)

    columns = [[at_latitude(value, a) for a in range(3)] for value in columns]

    west = sum(dot(columns[1][a][0:lat], tap(3 * a)) for a in range(3))
    east = sum(dot(columns[1][a][lat : 2 * lat], tap(3 * a + 2)) for a in range(3))
    rows = 8 * lon
    column = lax.broadcasted_iota(jnp.int32, (rows, ch), 0) & (lon - 1)
    for step in range(lat // 8):
        at = slice(step * rows, (step + 1) * rows)
        preact = preact_ref[at, :]
        preact += jnp.where(column == 0, spread(west, step, lon), 0.0)
        preact += jnp.where(column == lon - 1, spread(east, step, lon), 0.0)
        out, slope = swish(preact, cot_ref[at, :].astype(F32))
        out_ref[at, :] = out.astype(BF16)
        slope_ref[at, :] = slope.astype(BF16)
    out_copy = pltpu.make_async_copy(out_ref, out_hbm, out_sem)
    out_copy.start()

    total = jnp.zeros((2 * lat, ch), F32)
    for a in range(3):
        for b in range(3):
            total += dot(columns[b][a], tap(3 * a + b))
    upstream = jnp.concatenate([left_ref[2].astype(F32), right_ref[2].astype(F32)], 0)
    edge_ref[...] = swish(total, upstream)[1].astype(BF16)

    own_edge = picked((0, lon - 1), slope_ref, lat, lon)
    for k in range(9):
        a, b = k // 3, k % 3
        term = dot(x_wide[a * lon : a * lon + cells, b * ch : (b + 1) * ch], slope_ref[...], TN)
        if b == 0:
            term += dot(columns[1][a][0:lat], own_edge[0:lat], TN)
        if b == 2:
            term += dot(columns[1][a][lat : 2 * lat], own_edge[lat : 2 * lat], TN)
        wgrad_ref[k * ch : (k + 1) * ch, :] = (term * scale).astype(BF16)
    pairs, piece, _ = keep_ref.shape
    for pair in range(pairs):
        for held, owner in ((keep_ref, core), (send_ref, 1 - core)):
            start = pl.multiple_of((2 * pair + owner) * piece, 16)
            held[pair] = wgrad_ref[pl.ds(start, piece), :]
    out_copy.wait()


def conv_call(x, upstream, kernel, lat, lon, tiles, rows_dev, scale):
    cells, ch = x.shape
    kernel_rows = kernel.shape[0]
    sds, local = jax.ShapeDtypeStruct, pltpu.VMEM
    image = local((cells, ch), BF16)
    edges = local((3, lat, ch), BF16)
    x, upstream, kernel, east, west = pl.pallas_call(
        functools.partial(load_kernel, lat, lon),
        out_shape=(image, image, local((kernel_rows, ch), BF16), edges, edges),
        in_specs=[HBM] * 3,
        out_specs=(VMEM,) * 5,
        scratch_shapes=[pltpu.SemaphoreType.DMA((3,))],
        compiler_params=pltpu.CompilerParams(vmem_limit_bytes=WHOLE),
        name="load",
    )(x, upstream, kernel)
    left = lax.ppermute(east, "tile", shift("tile", 1))
    right = lax.ppermute(west, "tile", shift("tile", -1))
    wide, preact = pl.pallas_call(
        functools.partial(inner_kernel, lat, lon),
        out_shape=(local((cells + 2 * lon, 3 * ch), BF16), local((cells, ch), F32)),
        in_specs=[VMEM] * 2,
        out_specs=(VMEM,) * 2,
        compiler_params=pltpu.CompilerParams(vmem_limit_bytes=BIG),
        cost_estimate=pl.CostEstimate(
            flops=2 * cells * kernel_rows * ch, bytes_accessed=0, transcendentals=0
        ),
        name="inner",
    )(x, kernel)
    half = local((tiles // 2, rows_dev, ch), BF16)
    out, slope, edge, keep, send = pl.pallas_call(
        functools.partial(conv_kernel, lat, lon, scale),
        out_shape=(sds((cells, ch), BF16), image, local((2 * lat, ch), BF16), half, half),
        in_specs=[VMEM] * 8,
        out_specs=(HBM,) + (VMEM,) * 4,
        scratch_shapes=[
            pltpu.VMEM((cells, ch), BF16),
            pltpu.VMEM((kernel_rows, ch), BF16),
            pltpu.SemaphoreType.DMA,
        ],
        compiler_params=pltpu.CompilerParams(vmem_limit_bytes=BIG),
        cost_estimate=pl.CostEstimate(
            flops=2 * cells * kernel_rows * ch, bytes_accessed=2**20, transcendentals=cells * ch
        ),
        name="conv",
    )(wide, preact, upstream, kernel, east, west, left, right)
    return out, slope, edge, keep, send, kernel


def input_grad_kernel(lat, lon, slope_ref, edge_ref, w_ref, xgrad_ref, s_wide):
    cells, ch = slope_ref.shape
    chunk = cells // 2
    edge = edge_ref[...].astype(F32)
    widen(slope_ref, edge[:lat], edge[lat:], s_wide, lat, lon, 2, 0)

    def input_grad(step, carry):
        at = pl.multiple_of(step * chunk, chunk)
        total = None
        for a in range(3):
            for b in range(3):
                tap = 3 * a + b
                term = dot(
                    s_wide[pl.ds(at + (2 - a) * lon, chunk), b * ch : (b + 1) * ch],
                    w_ref[tap * ch : (tap + 1) * ch, :],
                    NT,
                )
                total = term if total is None else total + term
        xgrad_ref[pl.ds(at, chunk), :] = total.astype(BF16)
        return carry

    lax.fori_loop(0, cells // chunk, input_grad, 0)


def matrix_kernel(wgrad_ref, error_ref, q_ref, matrix_ref, p_ref):
    matrix = wgrad_ref[0].astype(F32)
    for t in range(1, wgrad_ref.shape[0]):
        matrix += wgrad_ref[t].astype(F32)
    matrix += error_ref[...]
    matrix_ref[...] = matrix
    q_parts = stacked_parts(q_ref[...])
    p_rows = jnp.zeros(p_ref.shape, F32)
    for part in in_parts(matrix):
        p_rows += fold(dot(q_parts, part, NT), q_ref.shape[0])
    p_ref[...] = p_rows


def moment_kernel(matrix_ref, p_ref, rows_ref, moment_ref):
    images, rank, rows = p_ref.shape
    ch = matrix_ref.shape[1]
    p_rows = p_ref[0]
    for image in range(1, images):
        p_rows += p_ref[image]
    p_rows = p_rows * (1.0 / images)
    rows_ref[...] = p_rows
    p_parts = stacked_parts(p_rows)
    moment = jnp.zeros((rank, ch), F32)
    for part in in_parts(matrix_ref[...]):
        moment += fold(dot(p_parts, part), rank)
    moment_ref[:, 0:ch] = moment
    gram = jnp.zeros((rank, 128), F32)
    for part in in_parts(p_rows):
        padded = jnp.concatenate([part.astype(F32), jnp.zeros((128 - rank, rows), F32)], 0)
        gram += fold(dot(p_parts, padded.astype(BF16), NT), rank)
    moment_ref[:, ch : ch + 128] = gram


def factor_kernel(gram_ref, p_ref, left_ref, held_ref, solve_ref):
    rank = p_ref.shape[0]
    gram = gram_ref[...]
    p_rows = p_ref[...]
    index = lax.broadcasted_iota(jnp.int32, (rank, 1), 0)
    lane = lax.broadcasted_iota(jnp.int32, (rank, 128), 1)
    solve = jnp.where(lane == index, 1.0, 0.0)
    for j in range(rank):
        floor = 1e-14 * gram_ref[j : j + 1, j : j + 1]
        inverse = 1.0 / jnp.sqrt(jnp.maximum(gram[j : j + 1, j : j + 1], floor))
        projected = jnp.where(index > j, gram[:, j : j + 1] * inverse, 0.0)

        def step(value):
            unit = value[j : j + 1, :] * inverse
            return jnp.where(index == j, unit, value - projected * unit)

        gram, p_rows, solve = step(gram), step(p_rows), step(solve)
    left_ref[...] = p_rows
    held_ref[...] = p_rows
    solve_ref[...] = solve


def residual_kernel(matrix_ref, left_ref, solve_ref, s_ref, next_ref, right_ref):
    images, rank, _ = s_ref.shape
    mean = s_ref[0]
    for image in range(1, images):
        mean += s_ref[image]
    mean = mean * (1.0 / images)
    solve = solve_ref[...]
    right = solve[:, 0:1] * mean[0:1, :]
    for k in range(1, rank):
        right += solve[:, k : k + 1] * mean[k : k + 1, :]
    right_ref[...] = right
    columns = left_ref[...].T
    total = matrix_ref[...]
    for k in range(rank):
        total -= columns[:, k : k + 1] * right[k : k + 1, :]
    next_ref[...] = total


def shift(axis, step):
    count = lax.axis_size(axis)
    return [(i, (i + step) % count) for i in range(count)]


def cores(axis):
    return [(i, i ^ 1) for i in range(lax.axis_size(axis))]


def chips(axis):
    count = lax.axis_size(axis)
    return [list(range(core, count, 2)) for core in range(2)]


def shares_of(value, axis):
    count = lax.axis_size(axis)
    return lax.all_to_all(
        jnp.broadcast_to(value[None], (count,) + value.shape), axis, 0, 0, tiled=True
    )


def per_device(inputs, kernel, cotangent, feedback, q_start):
    _, lat, lon, ch = inputs.shape
    kernel_rows = kernel.shape[0]
    rows_dev = feedback.shape[1]
    rank = q_start.shape[1]
    cells = lat * lon
    tiles = lax.axis_size("tile")
    scale = 1.0 / math.sqrt(cells * tiles)
    x, upstream, error = inputs[0], cotangent[0], feedback[0]

    x_cells, upstream_cells = x.reshape(cells, ch), upstream.reshape(cells, ch)
    sds, local = jax.ShapeDtypeStruct, pltpu.VMEM
    out, slope, edge, keep, send, held_kernel = conv_call(
        x_cells, upstream_cells, kernel, lat, lon, tiles, rows_dev, scale
    )
    xgrad = pl.pallas_call(
        functools.partial(input_grad_kernel, lat, lon),
        out_shape=sds((cells, ch), BF16),
        in_specs=[VMEM] * 3,
        out_specs=VMEM,
        scratch_shapes=[pltpu.VMEM((cells + 2 * lon, 3 * ch), BF16)],
        compiler_params=pltpu.CompilerParams(vmem_limit_bytes=BIG),
        cost_estimate=pl.CostEstimate(
            flops=2 * cells * kernel_rows * ch, bytes_accessed=2 * 2**20, transcendentals=0
        ),
        name="input_grad",
    )(slope, edge, held_kernel)

    summed = keep + lax.ppermute(send, "tile", cores("tile"))
    wgrad_rows = lax.all_to_all(
        summed, "tile", 0, 0, axis_index_groups=chips("tile"), tiled=True
    )
    small = pltpu.CompilerParams(vmem_limit_bytes=16 * 2**20)
    matrix, p_local = pl.pallas_call(
        matrix_kernel,
        out_shape=(local((rows_dev, ch), F32), local((rank, rows_dev), F32)),
        in_specs=[VMEM] * 3,
        out_specs=(VMEM,) * 2,
        compiler_params=small,
        name="matrix",
    )(wgrad_rows, error, q_start.T)
    p_rows, moment = pl.pallas_call(
        moment_kernel,
        out_shape=(sds((rank, rows_dev), F32), sds((rank, ch + 128), F32)),
        in_specs=[VMEM] * 2,
        out_specs=(VMEM,) * 2,
        compiler_params=small,
        name="moment",
    )(matrix, shares_of(p_local, "dp"))
    moment = shares_of(moment, "tile").sum(0)
    p_factor, held_factor, solve = pl.pallas_call(
        factor_kernel,
        out_shape=(
            sds((rank, rows_dev), F32),
            local((rank, rows_dev), F32),
            local((rank, 128), F32),
        ),
        in_specs=[VMEM] * 2,
        out_specs=(VMEM,) * 3,
        compiler_params=small,
        name="factor",
    )(moment[:, ch:], p_rows)
    new_feedback, q_factor = pl.pallas_call(
        residual_kernel,
        out_shape=(sds((rows_dev, ch), F32), sds((rank, ch), F32)),
        in_specs=[VMEM] * 4,
        out_specs=(VMEM,) * 2,
        compiler_params=small,
        name="residual",
    )(matrix, held_factor, solve, shares_of(moment[:, :ch], "dp"))

    shape = inputs.shape
    return (out.reshape(shape), xgrad.reshape(shape), p_factor.T, q_factor.T, new_feedback[None])


def solution(mesh):
    in_specs = (
        P("dp", None, "tile", None),
        P(),
        P("dp", None, "tile", None),
        P("dp", "tile", None),
        P(),
    )
    out_specs = (
        P("dp", None, "tile", None),
        P("dp", None, "tile", None),
        P("tile", None),
        P(),
        P("dp", "tile", None),
    )
    return jax.shard_map(
        per_device, mesh=mesh, in_specs=in_specs, out_specs=out_specs, check_vma=False
    )
```

time: 121 us -> 99 us (0.82)
  between operations: 14.2 us -> 0.73 us
  blocking collectives: 63.8 us -> 59 us
  starting transfers between devices: 11.9 us -> 16.2 us
  waiting for transfers between devices: 12.4 us -> 8.3 us
  local copies, waits for them, and re-layouts: 4.79 us -> 0.79 us
    all_to_all x3 -> x2, blocking collectives: 48.1 us -> 35.5 us  [shares_of(): lax.all_to_all(jnp.broadcast_to(value[None], (count,) + value.shape), axi...]
    all_to_all x1, blocking collectives: 15.7 us -> 23.5 us  [per_device(): lax.all_to_all(summed, 'tile', 0, 0, axis_index_groups=chips('tile'), til...]
    ppermute x2 -> x3, starting transfers between devices: 6.91 us -> 11.9 us  [the longest x1 5 us: per_device(): summed = keep + lax.ppermute(send, 'tile', cores('tile'))]
    unnamed x16 -> x4, local copies, waits for them, and re-layouts: 4.01 us -> 0.01 us
    ppermute x2 -> x3, waiting for transfers between devices: 3.82 us -> 1.61 us  [the longest x1 1.61 us: per_device(): summed = keep + lax.ppermute(send, 'tile', cores('tile'))]
    all_to_all x1, waiting for transfers between devices: 8.58 us -> 6.69 us  [shares_of(): lax.all_to_all(jnp.broadcast_to(value[None], (count,) + value.shape), axi...]
    pallas_call x3 -> x8, Pallas kernels: 11.6 us -> 12.4 us  [the longest x1 3.45 us: conv_call(): pl.pallas_call(functools.partial(conv_kernel, lat, lon, scale), out_shape...]
  transfers between devices with their start and end apart: 4 -> 4, of which waited for: 3 -> 2; matrix products, arithmetic and copies ran while one was open for 1% -> 0% of each run, Pallas kernels for 3% -> 6%
where the time goes in v2:
time: 99 us; the launch traced here: 97.5 us
  blocking collectives  59 us (60%)
  starting transfers between devices  16.2 us (16%)
  Pallas kernels  12.4 us (13%)
  waiting for transfers between devices  8.3 us (8%)
    all_to_all x2, blocking collectives, shares_of(): lax.all_to_all(jnp.broadcast_to(value[None], (count,) + value.shape), axi...  35.5 us
    all_to_all x1, blocking collectives, per_device(): lax.all_to_all(summed, 'tile', 0, 0, axis_index_groups=chips('tile'), til...  23.5 us
    all_to_all x1, waiting for transfers between devices, shares_of(): lax.all_to_all(jnp.broadcast_to(value[None], (count,) + value.shape), axi...  6.69 us
    ppermute x1, starting transfers between devices, per_device(): summed = keep + lax.ppermute(send, 'tile', cores('tile'))  5 us
    all_to_all x1, starting transfers between devices, shares_of(): lax.all_to_all(jnp.broadcast_to(value[None], (count,) + value.shape), axi...  4.28 us
    ppermute x1, starting transfers between devices, conv_call(): left = lax.ppermute(east, 'tile', shift('tile', 1))  3.49 us
    pallas_call x1, Pallas kernels, conv_call(): pl.pallas_call(functools.partial(conv_kernel, lat, lon, scale), out_shape...  3.45 us
    ppermute x1, starting transfers between devices, conv_call(): right = lax.ppermute(west, 'tile', shift('tile', -1))  3.42 us
  transfers between devices with their start and end apart: 4, of which 2 were waited for; matrix products, arithmetic and copies ran while one was open for 0% of the time, Pallas kernels for 6%

profile of v2, /device:TPU:1, one launch (start us, length us, event | category | flops | bytes accessed | tf_op | source)
XLA Modules:
  0.0 97.5 jit_solution(4440306883733910098)
XLA Ops:
  0.6 1.6 %load.1 = (bf16[1024,256]{1,0:T(8,128)(2,1)S(1)}, bf16[1024,256]{1,0:T(8,128)(2,1)S(1)}, bf16[2304,256]{1,0:T(8,128)(2,1)S(1)}, bf16[3,32,256]{2,1,0:T(8,128)(2,1)S(1)}, bf16[3,32,256]{2,1,0:T(8,128)(2,1)S(1)}) custom-call(bf16[1024,256]{1,0:T(8,128)(2,1)} %bitcast.11, bf16[1024,256]{1,0:T(8,128)(2,1)} %bitcast.12, bf16[2304,256]{1,0:T(8,128)(2,1)} %w_hbm.1), custom_call_target="tpu_custom_call" | custom-call | tf_op jit(solution)/shard_map/load/pallas_call | solution.py:196
  2.3 3.5 %collective-permute-start = (bf16[3,32,256]{2,1,0:T(8,128)(2,1)S(1)}, bf16[3,32,256]{2,1,0:T(8,128)(2,1)S(1)}, u32[]{:S(2)}, u32[]{:S(2)}) collective-permute-start(bf16[3,32,256]{2,1,0:T(8,128)(2,1)S(1)} %get-tuple-element.31.east_ref), channel_id=1, source_target_pairs={{0,1},{1,2},{2,3},{3,4},{4,5},{5,6},{6,7},{7,8},{8,9},{9,10},{10,1... | collective-permute-start | bytes 147464 | tf_op jit(solution)/shard_map/ppermute | solution.py:205
  5.8 3.4 %collective-permute-start.1 = (bf16[3,32,256]{2,1,0:T(8,128)(2,1)S(1)}, bf16[3,32,256]{2,1,0:T(8,128)(2,1)S(1)}, u32[]{:S(2)}, u32[]{:S(2)}) collective-permute-start(bf16[3,32,256]{2,1,0:T(8,128)(2,1)S(1)} %get-tuple-element.32.west_ref), channel_id=1, source_target_pairs={{0,15},{1,0},{2,1},{3,2},{4,3},{5,4},{6,5},{7,6},{8,7},{9,8},{10,9... | collective-permute-start | bytes 147464 | tf_op jit(solution)/shard_map/ppermute | solution.py:206
  9.2 1.8 %inner.1 = (bf16[1088,768]{1,0:T(8,128)(2,1)S(1)}, f32[1024,256]{1,0:T(8,128)S(1)}) custom-call(bf16[1024,256]{1,0:T(8,128)(2,1)S(1)} %get-tuple-element.26.x_ref, bf16[2304,256]{1,0:T(8,128)(2,1)S(1)} %get-tuple-element.27.w_ref), custom_call_target="tpu_custom_call" | custom-call | flops 1207959552 | tf_op jit(solution)/shard_map/inner/pallas_call | solution.py:207
  11.0 0.0 collective-permute-done.left_ref
  11.0 0.0 collective-permute-done.1.right_ref
  11.0 3.4 %conv.1 = (bf16[1024,256]{1,0:T(8,128)(2,1)}, bf16[1024,256]{1,0:T(8,128)(2,1)S(1)}, bf16[64,256]{1,0:T(8,128)(2,1)S(1)}, bf16[8,144,256]{2,1,0:T(8,128)(2,1)S(1)}, bf16[8,144,256]{2,1,0:T(8,128)(2,1)S(1)}) custom-call(bf16[1088,768]{1,0:T(8,128)(2,1)S(1)} %get-tuple-element.28.x_wide, f32[1024,256]{1,0:T(8,128)S(1)} %get-tuple-element.29.preact_ref, ...), custom_call_target="tpu_custom_call" | custom-call | flops 1207959552 | bytes 1048576 | tf_op jit(solution)/shard_map/conv/pallas_call | solution.py:219
  14.5 5.0 %collective-permute-start.2 = (bf16[8,144,256]{2,1,0:T(8,128)(2,1)S(1)}, bf16[8,144,256]{2,1,0:T(8,128)(2,1)S(1)}, u32[]{:S(2)}, u32[]{:S(2)}) collective-permute-start(bf16[8,144,256]{2,1,0:T(8,128)(2,1)S(1)} %get-tuple-element.37), channel_id=1, source_target_pairs={{0,1},{1,0},{2,3},{3,2},{4,5},{5,4},{6,7},{7,6},{8,9},{9,8},{10,11... | collective-permute-start | bytes 1769480 | tf_op jit(solution)/shard_map/ppermute | solution.py:384
  19.5 1.6 %collective-permute-done.2 = bf16[8,144,256]{2,1,0:T(8,128)(2,1)S(1)} collective-permute-done((bf16[8,144,256]{2,1,0:T(8,128)(2,1)S(1)}, bf16[8,144,256]{2,1,0:T(8,128)(2,1)S(1)}, u32[]{:S(2)}, u32[]{:S(2)}) %collective-permute-start.2) | collective-permute-done | bytes 589856 | tf_op jit(solution)/shard_map/ppermute | solution.py:384
  21.1 0.0 copy-start
  21.1 0.0 copy-start.1
  21.1 0.1 add.3
  21.3 23.5 %all_to_all.20.wgrad_ref = bf16[8,144,256]{2,1,0:T(8,128)(2,1)S(1)} all-to-all(bf16[8,144,256]{2,1,0:T(8,128)(2,1)S(1)} %add.3), channel_id=1, replica_groups={{0,2,4,6,8,10,12,14},{1,3,5,7,9,11,13,15},{16,18,20,22,24,26,28,30},{17..., dimensions={0} | all-to-all | bytes 1179648 | tf_op jit(solution)/shard_map/all_to_all | solution.py:385
  44.7 0.0 copy-done
  44.7 0.0 copy-done.1
  44.7 0.2 matrix.1
  45.0 19.1 %all_to_all.21.p_ref = f32[32,8,144]{2,1,0:T(8,128)S(1)} all-to-all(f32[32,8,144]{2,1,0:T(8,128)S(1)} %broadcast_in_dim.8), channel_id=1, replica_groups=mesh['dp'=32,'tile'=16] {'dp'}, dimensions={0} | all-to-all | bytes 294912 | tf_op jit(solution)/shard_map/all_to_all | solution.py:351
  64.2 0.2 moment.1
  64.4 16.4 %all_to_all.22 = f32[16,8,384]{2,1,0:T(8,128)S(1)} all-to-all(f32[16,8,384]{2,1,0:T(8,128)S(1)} %broadcast_in_dim.9), channel_id=1, replica_groups=mesh['dp'=32,'tile'=16] {'tile'}, dimensions={0} | all-to-all | bytes 393216 | tf_op jit(solution)/shard_map/all_to_all | solution.py:351
  80.8 0.7 broadcast_in_dim.10
  81.5 4.3 %all-to-all-start.3 = ((f32[32,8,256]{2,1,0:T(8,128)}), f32[32,8,256]{2,1,0:T(8,128)S(1)}, u32[]{:S(2)}, u32[]{:S(2)}) async-start(f32[32,8,256]{2,1,0:T(8,128)} %broadcast_in_dim.10), calls=%async_computation.3 | async-start | bytes 524288 | tf_op jit(solution)/shard_map/all_to_all | solution.py:351
  85.8 2.7 %input_grad.1 = bf16[1024,256]{1,0:T(8,128)(2,1)} custom-call(bf16[1024,256]{1,0:T(8,128)(2,1)S(1)} %get-tuple-element.34.slope_ref, bf16[64,256]{1,0:T(8,128)(2,1)S(1)} %get-tuple-element.35.edge_ref, bf16[2304,256]{1,0:T(8,128)(2,1)S(1)} %get-tuple-element.27.w_ref), custom_call_target="tpu_custom_call" | custom-call | flops 1207959552 | bytes 2097152 | tf_op jit(solution)/shard_map/input_grad/pallas_call | solution.py:371
  88.5 1.3 %factor.1 = (f32[8,144]{1,0:T(8,128)}, f32[8,144]{1,0:T(8,128)S(1)}, f32[8,128]{1,0:T(8,128)S(1)}) custom-call(f32[8,128]{1,0:T(8,128)S(1)} %slice.8.gram_ref, f32[8,144]{1,0:T(8,128)S(1)} %get-tuple-element.41.p_ref), custom_call_target="tpu_custom_call" | custom-call | tf_op jit(solution)/shard_map/factor/pallas_call | solution.py:406
  89.8 6.7 %all-to-all-done.3.s_ref = f32[32,8,256]{2,1,0:T(8,128)S(1)} async-done(((f32[32,8,256]{2,1,0:T(8,128)}), f32[32,8,256]{2,1,0:T(8,128)S(1)}, u32[]{:S(2)}, u32[]{:S(2)}) %all-to-all-start.3) | async-done | bytes 262176 | tf_op jit(solution)/shard_map/all_to_all | solution.py:351
  96.5 1.0 %residual.1 = (f32[144,256]{1,0:T(8,128)}, f32[8,256]{1,0:T(8,128)}) custom-call(f32[144,256]{1,0:T(8,128)S(1)} %get-tuple-element.38.matrix_ref, f32[8,144]{1,0:T(8,128)S(1)} %get-tuple-element.43.left_ref, f32[8,128]{1,0:T(8,128)S(1)} %get-tuple-element.44.solve_ref, f32[32,8,256]{2,1,0:T(8,128)S(1)} %all-to-all-done.3.s_ref), custom_call_target="tpu_custom_call" | custom-call | tf_op jit(solution)/shard_map/residual/pallas_call | solution.py:418
  (5 shorter events, 0.1 us)
Async XLA Ops:
  2.3 8.8 %collective-permute-start = (bf16[3,32,256]{2,1,0:T(8,128)(2,1)S(1)}, bf16[3,32,256]{2,1,0:T(8,128)(2,1)S(1)}, u32[]{:S(2)}, u32[]{:S(2)}) collective-permute-start(bf16[3,32,256]{2,1,0:T(8,128)(2,1)S(1)} %get-tuple-element.31.east_ref), channel_id=1, source_target_pairs={{0,1},{1,2},{2,3},{3,4},{4,5},{5,6},{6,7},{7,8},{8,9},{9,10},{10,1... | collective-permute-start | bytes 147464 | tf_op jit(solution)/shard_map/ppermute | solution.py:205
  5.8 5.3 %collective-permute-start.1 = (bf16[3,32,256]{2,1,0:T(8,128)(2,1)S(1)}, bf16[3,32,256]{2,1,0:T(8,128)(2,1)S(1)}, u32[]{:S(2)}, u32[]{:S(2)}) collective-permute-start(bf16[3,32,256]{2,1,0:T(8,128)(2,1)S(1)} %get-tuple-element.32.west_ref), channel_id=1, source_target_pairs={{0,15},{1,0},{2,1},{3,2},{4,3},{5,4},{6,5},{7,6},{8,7},{9,8},{10,9... | collective-permute-start | bytes 147464 | tf_op jit(solution)/shard_map/ppermute | solution.py:206
  14.5 6.6 %collective-permute-start.2 = (bf16[8,144,256]{2,1,0:T(8,128)(2,1)S(1)}, bf16[8,144,256]{2,1,0:T(8,128)(2,1)S(1)}, u32[]{:S(2)}, u32[]{:S(2)}) collective-permute-start(bf16[8,144,256]{2,1,0:T(8,128)(2,1)S(1)} %get-tuple-element.37), channel_id=1, source_target_pairs={{0,1},{1,0},{2,3},{3,2},{4,5},{5,4},{6,7},{7,6},{8,9},{9,8},{10,11... | collective-permute-start | bytes 1769480 | tf_op jit(solution)/shard_map/ppermute | solution.py:384
  21.1 23.6 %copy-start = (f32[1,144,256]{2,1,0:T(8,128)S(1)}, f32[1,144,256]{2,1,0:T(8,128)}, u32[]{:S(2)}) copy-start(f32[1,144,256]{2,1,0:T(8,128)} %param.8) | copy-start | bytes 442372
  21.1 23.6 %copy-start.1 = (f32[256,8]{0,1:T(8,128)S(1)}, f32[256,8]{0,1:T(8,128)}, u32[]{:S(2)}) copy-start(f32[256,8]{0,1:T(8,128)} %param.9) | copy-start | bytes 24580
  81.5 15.0 %all-to-all-start.3 = ((f32[32,8,256]{2,1,0:T(8,128)}), f32[32,8,256]{2,1,0:T(8,128)S(1)}, u32[]{:S(2)}, u32[]{:S(2)}) async-start(f32[32,8,256]{2,1,0:T(8,128)} %broadcast_in_dim.10), calls=%async_computation.3 | async-start | bytes 524288 | tf_op jit(solution)/shard_map/all_to_all | solution.py:351

commit v3 on v2

--- a/solution.py
+++ b/solution.py
@@ -121,35 +121,26 @@
     lax.fori_loop(0, cells // chunk, forward, 0)
 
 
+def shifted(west, east, lat):
+    value = jnp.concatenate([west.astype(F32), east.astype(F32)], 0)
+    row = lax.broadcasted_iota(jnp.int32, value.shape, 0) & (lat - 1)
+    south = jnp.where(row == 0, 0.0, pltpu.roll(value, 1, 0))
+    north = jnp.where(row == lat - 1, 0.0, pltpu.roll(value, 2 * lat - 1, 0))
+    return [south.astype(BF16), value.astype(BF16), north.astype(BF16)]
+
+
 def conv_kernel(
-    lat, lon, scale, x_wide, preact_ref, cot_ref, w_ref, east_ref, west_ref, left_ref, right_ref,
-    out_hbm, slope_ref, edge_ref, keep_ref, send_ref, out_ref, wgrad_ref, out_sem,
+    lat, lon, scale, x_wide, preact_ref, cot_ref, w_ref, left_ref, right_ref,
+    out_ref, slope_ref, keep_ref, send_ref, x_sides, wgrad_ref,
 ):
     cells, ch = cot_ref.shape
     core = lax.axis_index("tile") & 1
     tap = lambda k: w_ref[k * ch : (k + 1) * ch, :]
 
-    columns = [
-        jnp.concatenate([west.astype(F32), east.astype(F32)], 0)
-        for west, east in (
-            (left_ref[0], east_ref[1]),
-            (left_ref[1], right_ref[0]),
-            (west_ref[0], right_ref[1]),
-        )
-    ]
-    row = lax.broadcasted_iota(jnp.int32, (2 * lat, ch), 0) & (lat - 1)
-
-    def at_latitude(value, a):
-        if a == 0:
-            value = jnp.where(row == 0, 0.0, pltpu.roll(value, 1, 0))
-        if a == 2:
-            value = jnp.where(row == lat - 1, 0.0, pltpu.roll(value, 2 * lat - 1, 0))
-        return value.astype(BF16)
-
-    columns = [[at_latitude(value, a) for a in range(3)] for value in columns]
-
-    west = sum(dot(columns[1][a][0:lat], tap(3 * a)) for a in range(3))
-    east = sum(dot(columns[1][a][lat : 2 * lat], tap(3 * a + 2)) for a in range(3))
+    beside = shifted(left_ref[1], right_ref[0], lat)
+
+    west = sum(dot(beside[a][0:lat], tap(3 * a)) for a in range(3))
+    east = sum(dot(beside[a][lat : 2 * lat], tap(3 * a + 2)) for a in range(3))
     rows = 8 * lon
     column = lax.broadcasted_iota(jnp.int32, (rows, ch), 0) & (lon - 1)
     for step in range(lat // 8):
@@ -160,31 +151,26 @@
         out, slope = swish(preact, cot_ref[at, :].astype(F32))
         out_ref[at, :] = out.astype(BF16)
         slope_ref[at, :] = slope.astype(BF16)
-    out_copy = pltpu.make_async_copy(out_ref, out_hbm, out_sem)
-    out_copy.start()
-
-    total = jnp.zeros((2 * lat, ch), F32)
-    for a in range(3):
-        for b in range(3):
-            total += dot(columns[b][a], tap(3 * a + b))
-    upstream = jnp.concatenate([left_ref[2].astype(F32), right_ref[2].astype(F32)], 0)
-    edge_ref[...] = swish(total, upstream)[1].astype(BF16)
-
-    own_edge = picked((0, lon - 1), slope_ref, lat, lon)
+        wide_at = slice(lon + step * rows, lon + (step + 1) * rows)
+        for side, place, edge in ((0, 0, left_ref[1]), (1, lon - 1, right_ref[0])):
+            value = x_wide[wide_at, 2 * side * ch : (2 * side + 1) * ch].astype(F32)
+            value = jnp.where(column == place, spread(edge.astype(F32), step, lon), value)
+            x_sides[wide_at, side * ch : (side + 1) * ch] = value.astype(BF16)
+    x_sides[0:lon, :] = jnp.zeros((lon, 2 * ch), BF16)
+    x_sides[lon + cells :, :] = jnp.zeros((lon, 2 * ch), BF16)
+
     for k in range(9):
         a, b = k // 3, k % 3
-        term = dot(x_wide[a * lon : a * lon + cells, b * ch : (b + 1) * ch], slope_ref[...], TN)
-        if b == 0:
-            term += dot(columns[1][a][0:lat], own_edge[0:lat], TN)
-        if b == 2:
-            term += dot(columns[1][a][lat : 2 * lat], own_edge[lat : 2 * lat], TN)
+        source, block = (x_wide, 1) if b == 1 else (x_sides, b // 2)
+        term = dot(
+            source[a * lon : a * lon + cells, block * ch : (block + 1) * ch], slope_ref[...], TN
+        )
         wgrad_ref[k * ch : (k + 1) * ch, :] = (term * scale).astype(BF16)
     pairs, piece, _ = keep_ref.shape
     for pair in range(pairs):
         for held, owner in ((keep_ref, core), (send_ref, 1 - core)):
             start = pl.multiple_of((2 * pair + owner) * piece, 16)
             held[pair] = wgrad_ref[pl.ds(start, piece), :]
-    out_copy.wait()
 
 
 def conv_call(x, upstream, kernel, lat, lon, tiles, rows_dev, scale):
@@ -216,29 +202,41 @@
         name="inner",
     )(x, kernel)
     half = local((tiles // 2, rows_dev, ch), BF16)
-    out, slope, edge, keep, send = pl.pallas_call(
+    out, slope, keep, send = pl.pallas_call(
         functools.partial(conv_kernel, lat, lon, scale),
-        out_shape=(sds((cells, ch), BF16), image, local((2 * lat, ch), BF16), half, half),
-        in_specs=[VMEM] * 8,
-        out_specs=(HBM,) + (VMEM,) * 4,
+        out_shape=(image, image, half, half),
+        in_specs=[VMEM] * 6,
+        out_specs=(VMEM,) * 4,
         scratch_shapes=[
-            pltpu.VMEM((cells, ch), BF16),
+            pltpu.VMEM((cells + 2 * lon, 2 * ch), BF16),
             pltpu.VMEM((kernel_rows, ch), BF16),
-            pltpu.SemaphoreType.DMA,
         ],
         compiler_params=pltpu.CompilerParams(vmem_limit_bytes=BIG),
         cost_estimate=pl.CostEstimate(
             flops=2 * cells * kernel_rows * ch, bytes_accessed=2**20, transcendentals=cells * ch
         ),
         name="conv",
-    )(wide, preact, upstream, kernel, east, west, left, right)
-    return out, slope, edge, keep, send, kernel
-
-
-def input_grad_kernel(lat, lon, slope_ref, edge_ref, w_ref, xgrad_ref, s_wide):
+    )(wide, preact, upstream, kernel, left, right)
+    return out, slope, keep, send, (kernel, east, west, left, right)
+
+
+def input_grad_kernel(
+    lat, lon, slope_ref, w_ref, east_ref, west_ref, left_ref, right_ref, xgrad_ref, s_wide
+):
     cells, ch = slope_ref.shape
     chunk = cells // 2
-    edge = edge_ref[...].astype(F32)
+    columns = [
+        shifted(left_ref[0], east_ref[1], lat),
+        shifted(left_ref[1], right_ref[0], lat),
+        shifted(west_ref[0], right_ref[1], lat),
+    ]
+    total = jnp.zeros((2 * lat, ch), F32)
+    for a in range(3):
+        for b in range(3):
+            tap = 3 * a + b
+            total += dot(columns[b][a], w_ref[tap * ch : (tap + 1) * ch, :])
+    upstream = jnp.concatenate([left_ref[2].astype(F32), right_ref[2].astype(F32)], 0)
+    edge = swish(total, upstream)[1].astype(BF16).astype(F32)
     widen(slope_ref, edge[:lat], edge[lat:], s_wide, lat, lon, 2, 0)
 
     def input_grad(step, carry):
@@ -269,38 +267,47 @@
     p_rows = jnp.zeros(p_ref.shape, F32)
     for part in in_parts(matrix):
         p_rows += fold(dot(q_parts, part, NT), q_ref.shape[0])
-    p_ref[...] = p_rows
+    p_ref[...] = p_rows.astype(BF16)
+
+
+def image_mean(ref):
+    total = ref[0].astype(F32)
+    for image in range(1, ref.shape[0]):
+        total += ref[image].astype(F32)
+    return total * (1.0 / ref.shape[0])
 
 
 def moment_kernel(matrix_ref, p_ref, rows_ref, moment_ref):
-    images, rank, rows = p_ref.shape
+    _, rank, rows = p_ref.shape
     ch = matrix_ref.shape[1]
-    p_rows = p_ref[0]
-    for image in range(1, images):
-        p_rows += p_ref[image]
-    p_rows = p_rows * (1.0 / images)
+    p_rows = image_mean(p_ref)
     rows_ref[...] = p_rows
     p_parts = stacked_parts(p_rows)
     moment = jnp.zeros((rank, ch), F32)
     for part in in_parts(matrix_ref[...]):
         moment += fold(dot(p_parts, part), rank)
-    moment_ref[:, 0:ch] = moment
+    moment_ref[:, 0:ch] = moment.astype(BF16)
     gram = jnp.zeros((rank, 128), F32)
     for part in in_parts(p_rows):
-        padded = jnp.concatenate([part.astype(F32), jnp.zeros((128 - rank, rows), F32)], 0)
-        gram += fold(dot(p_parts, padded.astype(BF16), NT), rank)
-    moment_ref[:, ch : ch + 128] = gram
+        thrice = [part.astype(F32)] * 3 + [jnp.zeros((128 - 3 * rank, rows), F32)]
+        gram += fold(dot(p_parts, jnp.concatenate(thrice, 0).astype(BF16), NT), rank)
+    place = lax.broadcasted_iota(jnp.int32, (rank, 128), 1) // rank
+    parts = [part.astype(F32) for part in in_parts(gram)]
+    parts = jnp.where(place == 0, parts[0], jnp.where(place == 1, parts[1], parts[2]))
+    moment_ref[:, ch : ch + 128] = parts.astype(BF16)
 
 
 def factor_kernel(gram_ref, p_ref, left_ref, held_ref, solve_ref):
     rank = p_ref.shape[0]
     gram = gram_ref[...]
+    gram += pltpu.roll(gram, 128 - rank, 1) + pltpu.roll(gram, 128 - 2 * rank, 1)
+    whole = gram
     p_rows = p_ref[...]
     index = lax.broadcasted_iota(jnp.int32, (rank, 1), 0)
     lane = lax.broadcasted_iota(jnp.int32, (rank, 128), 1)
     solve = jnp.where(lane == index, 1.0, 0.0)
     for j in range(rank):
-        floor = 1e-14 * gram_ref[j : j + 1, j : j + 1]
+        floor = 1e-14 * whole[j : j + 1, j : j + 1]
         inverse = 1.0 / jnp.sqrt(jnp.maximum(gram[j : j + 1, j : j + 1], floor))
         projected = jnp.where(index > j, gram[:, j : j + 1] * inverse, 0.0)
 
@@ -315,11 +322,8 @@
 
 
 def residual_kernel(matrix_ref, left_ref, solve_ref, s_ref, next_ref, right_ref):
-    images, rank, _ = s_ref.shape
-    mean = s_ref[0]
-    for image in range(1, images):
-        mean += s_ref[image]
-    mean = mean * (1.0 / images)
+    rank = s_ref.shape[1]
+    mean = image_mean(s_ref)
     solve = solve_ref[...]
     right = solve[:, 0:1] * mean[0:1, :]
     for k in range(1, rank):
@@ -365,13 +369,13 @@
 
     x_cells, upstream_cells = x.reshape(cells, ch), upstream.reshape(cells, ch)
     sds, local = jax.ShapeDtypeStruct, pltpu.VMEM
-    out, slope, edge, keep, send, held_kernel = conv_call(
+    out, slope, keep, send, held = conv_call(
         x_cells, upstream_cells, kernel, lat, lon, tiles, rows_dev, scale
     )
     xgrad = pl.pallas_call(
         functools.partial(input_grad_kernel, lat, lon),
         out_shape=sds((cells, ch), BF16),
-        in_specs=[VMEM] * 3,
+        in_specs=[VMEM] * 6,
         out_specs=VMEM,
         scratch_shapes=[pltpu.VMEM((cells + 2 * lon, 3 * ch), BF16)],
         compiler_params=pltpu.CompilerParams(vmem_limit_bytes=BIG),
@@ -379,7 +383,7 @@
             flops=2 * cells * kernel_rows * ch, bytes_accessed=2 * 2**20, transcendentals=0
         ),
         name="input_grad",
-    )(slope, edge, held_kernel)
+    )(slope, *held)
 
     summed = keep + lax.ppermute(send, "tile", cores("tile"))
     wgrad_rows = lax.all_to_all(
@@ -388,7 +392,7 @@
     small = pltpu.CompilerParams(vmem_limit_bytes=16 * 2**20)
     matrix, p_local = pl.pallas_call(
         matrix_kernel,
-        out_shape=(local((rows_dev, ch), F32), local((rank, rows_dev), F32)),
+        out_shape=(local((rows_dev, ch), F32), local((rank, rows_dev), BF16)),
         in_specs=[VMEM] * 3,
         out_specs=(VMEM,) * 2,
         compiler_params=small,
@@ -396,13 +400,13 @@
     )(wgrad_rows, error, q_start.T)
     p_rows, moment = pl.pallas_call(
         moment_kernel,
-        out_shape=(sds((rank, rows_dev), F32), sds((rank, ch + 128), F32)),
+        out_shape=(local((rank, rows_dev), F32), local((rank, ch + 128), BF16)),
         in_specs=[VMEM] * 2,
         out_specs=(VMEM,) * 2,
         compiler_params=small,
         name="moment",
     )(matrix, shares_of(p_local, "dp"))
-    moment = shares_of(moment, "tile").sum(0)
+    moment = shares_of(moment, "tile").astype(F32).sum(0)
     p_factor, held_factor, solve = pl.pallas_call(
         factor_kernel,
         out_shape=(
@@ -422,7 +426,7 @@
         out_specs=(VMEM,) * 2,
         compiler_params=small,
         name="residual",
-    )(matrix, held_factor, solve, shares_of(moment[:, :ch], "dp"))
+    )(matrix, held_factor, solve, shares_of(moment[:, :ch].astype(BF16), "dp"))
 
     shape = inputs.shape
     return (out.reshape(shape), xgrad.reshape(shape), p_factor.T, q_factor.T, new_feedback[None])

time: 99 us -> 91.8 us (0.927); the launches traced: 97.5 us -> 91.5 us
  blocking collectives: 59 us -> 55.6 us
  waiting for transfers between devices: 8.3 us -> 5.74 us
    all_to_all x2, blocking collectives: 35.5 us -> 32.1 us  [shares_of(): lax.all_to_all(jnp.broadcast_to(value[None], (count,) + value.shape), axi...]
    all_to_all x1, waiting for transfers between devices: 6.69 us -> 4.12 us  [shares_of(): lax.all_to_all(jnp.broadcast_to(value[None], (count,) + value.shape), axi...]
  transfers between devices with their start and end apart: 4 -> 4, of which waited for: 2 -> 2; matrix products, arithmetic and copies ran while one was open for 0% -> 1% of each run, Pallas kernels for 6% -> 7%
where the time goes in v3:
time: 91.8 us; the launch traced here: 91.5 us
  blocking collectives  55.6 us (61%)
  starting transfers between devices  15.8 us (17%)
  Pallas kernels  11.9 us (13%)
  waiting for transfers between devices  5.74 us (6%)
  local copies, waits for them, and re-layouts  1.51 us (2%)
    all_to_all x2, blocking collectives, shares_of(): lax.all_to_all(jnp.broadcast_to(value[None], (count,) + value.shape), axi...  32.1 us
    all_to_all x1, blocking collectives, per_device(): lax.all_to_all(summed, 'tile', 0, 0, axis_index_groups=chips('tile'), til...  23.5 us
    ppermute x1, starting transfers between devices, per_device(): summed = keep + lax.ppermute(send, 'tile', cores('tile'))  5 us
    all_to_all x1, waiting for transfers between devices, shares_of(): lax.all_to_all(jnp.broadcast_to(value[None], (count,) + value.shape), axi...  4.12 us
    all_to_all x1, starting transfers between devices, shares_of(): lax.all_to_all(jnp.broadcast_to(value[None], (count,) + value.shape), axi...  3.86 us
    ppermute x1, starting transfers between devices, conv_call(): left = lax.ppermute(east, 'tile', shift('tile', 1))  3.49 us
    ppermute x1, starting transfers between devices, conv_call(): right = lax.ppermute(west, 'tile', shift('tile', -1))  3.42 us
    pallas_call x1, Pallas kernels, per_device(): pl.pallas_call(functools.partial(input_grad_kernel, lat, lon), out_shape=...  3.08 us
  transfers between devices with their start and end apart: 4, of which 2 were waited for; matrix products, arithmetic and copies ran while one was open for 1% of the time, Pallas kernels for 7%

profile of v3, /device:TPU:1, one launch (start us, length us, event | category | flops | bytes accessed | tf_op | source)
XLA Modules:
  0.0 91.5 jit_solution(6266781621062362384)
XLA Ops:
  0.6 1.6 %load.1 = (bf16[1024,256]{1,0:T(8,128)(2,1)S(1)}, bf16[1024,256]{1,0:T(8,128)(2,1)S(1)}, bf16[2304,256]{1,0:T(8,128)(2,1)S(1)}, bf16[3,32,256]{2,1,0:T(8,128)(2,1)S(1)}, bf16[3,32,256]{2,1,0:T(8,128)(2,1)S(1)}) custom-call(bf16[1024,256]{1,0:T(8,128)(2,1)} %bitcast.12, bf16[1024,256]{1,0:T(8,128)(2,1)} %bitcast.13, bf16[2304,256]{1,0:T(8,128)(2,1)} %w_hbm.1), custom_call_target="tpu_custom_call" | custom-call | tf_op jit(solution)/shard_map/load/pallas_call | solution.py:182
  2.3 3.5 %collective-permute-start = (bf16[3,32,256]{2,1,0:T(8,128)(2,1)S(1)}, bf16[3,32,256]{2,1,0:T(8,128)(2,1)S(1)}, u32[]{:S(2)}, u32[]{:S(2)}) collective-permute-start(bf16[3,32,256]{2,1,0:T(8,128)(2,1)S(1)} %get-tuple-element.30.east_ref), channel_id=1, source_target_pairs={{0,1},{1,2},{2,3},{3,4},{4,5},{5,6},{6,7},{7,8},{8,9},{9,10},{10,1... | collective-permute-start | bytes 147464 | tf_op jit(solution)/shard_map/ppermute | solution.py:191
  5.8 3.4 %collective-permute-start.1 = (bf16[3,32,256]{2,1,0:T(8,128)(2,1)S(1)}, bf16[3,32,256]{2,1,0:T(8,128)(2,1)S(1)}, u32[]{:S(2)}, u32[]{:S(2)}) collective-permute-start(bf16[3,32,256]{2,1,0:T(8,128)(2,1)S(1)} %get-tuple-element.31.west_ref), channel_id=1, source_target_pairs={{0,15},{1,0},{2,1},{3,2},{4,3},{5,4},{6,5},{7,6},{8,7},{9,8},{10,9... | collective-permute-start | bytes 147464 | tf_op jit(solution)/shard_map/ppermute | solution.py:192
  9.2 1.8 %inner.1 = (bf16[1088,768]{1,0:T(8,128)(2,1)S(1)}, f32[1024,256]{1,0:T(8,128)S(1)}) custom-call(bf16[1024,256]{1,0:T(8,128)(2,1)S(1)} %get-tuple-element.25.x_ref, bf16[2304,256]{1,0:T(8,128)(2,1)S(1)} %get-tuple-element.26.w_ref), custom_call_target="tpu_custom_call" | custom-call | flops 1207959552 | tf_op jit(solution)/shard_map/inner/pallas_call | solution.py:193
  11.0 0.0 collective-permute-done.left_ref
  11.0 0.0 collective-permute-done.1.right_ref
  11.0 2.5 %conv.1 = (bf16[1024,256]{1,0:T(8,128)(2,1)S(1)}, bf16[1024,256]{1,0:T(8,128)(2,1)S(1)}, bf16[8,144,256]{2,1,0:T(8,128)(2,1)S(1)}, bf16[8,144,256]{2,1,0:T(8,128)(2,1)S(1)}) custom-call(bf16[1088,768]{1,0:T(8,128)(2,1)S(1)} %get-tuple-element.27.x_wide, f32[1024,256]{1,0:T(8,128)S(1)} %get-tuple-element.28.preact_ref, ...), custom_call_target="tpu_custom_call" | custom-call | flops 1207959552 | bytes 1048576 | tf_op jit(solution)/shard_map/conv/pallas_call | solution.py:205
  13.6 5.0 %collective-permute-start.2 = (bf16[8,144,256]{2,1,0:T(8,128)(2,1)S(1)}, bf16[8,144,256]{2,1,0:T(8,128)(2,1)S(1)}, u32[]{:S(2)}, u32[]{:S(2)}) collective-permute-start(bf16[8,144,256]{2,1,0:T(8,128)(2,1)S(1)} %get-tuple-element.35), channel_id=1, source_target_pairs={{0,1},{1,0},{2,3},{3,2},{4,5},{5,4},{6,7},{7,6},{8,9},{9,8},{10,11... | collective-permute-start | bytes 1769480 | tf_op jit(solution)/shard_map/ppermute | solution.py:388
  18.6 1.6 %collective-permute-done.2 = bf16[8,144,256]{2,1,0:T(8,128)(2,1)S(1)} collective-permute-done((bf16[8,144,256]{2,1,0:T(8,128)(2,1)S(1)}, bf16[8,144,256]{2,1,0:T(8,128)(2,1)S(1)}, u32[]{:S(2)}, u32[]{:S(2)}) %collective-permute-start.2) | collective-permute-done | bytes 589856 | tf_op jit(solution)/shard_map/ppermute | solution.py:388
  20.2 0.0 copy-start
  20.2 0.0 copy-start.1
  20.2 0.1 add.3
  20.4 23.5 %all_to_all.20.wgrad_ref = bf16[8,144,256]{2,1,0:T(8,128)(2,1)S(1)} all-to-all(bf16[8,144,256]{2,1,0:T(8,128)(2,1)S(1)} %add.3), channel_id=1, replica_groups={{0,2,4,6,8,10,12,14},{1,3,5,7,9,11,13,15},{16,18,20,22,24,26,28,30},{17..., dimensions={0} | all-to-all | bytes 1179648 | tf_op jit(solution)/shard_map/all_to_all | solution.py:389
  43.8 0.0 copy-done
  43.8 0.0 copy-done.1
  43.8 0.2 matrix.1
  44.1 18.6 %all_to_all.21.p_ref = bf16[32,8,144]{2,1,0:T(8,128)(2,1)S(1)} all-to-all(bf16[32,8,144]{2,1,0:T(8,128)(2,1)S(1)} %broadcast_in_dim.8), channel_id=1, replica_groups=mesh['dp'=32,'tile'=16] {'dp'}, dimensions={0} | all-to-all | bytes 147456 | tf_op jit(solution)/shard_map/all_to_all | solution.py:355
  62.8 0.2 moment.1
  63.0 13.5 %all_to_all.22 = bf16[16,8,384]{2,1,0:T(8,128)(2,1)S(1)} all-to-all(bf16[16,8,384]{2,1,0:T(8,128)(2,1)S(1)} %broadcast_in_dim.9), channel_id=1, replica_groups=mesh['dp'=32,'tile'=16] {'tile'}, dimensions={0} | all-to-all | bytes 196608 | tf_op jit(solution)/shard_map/all_to_all | solution.py:355
  76.5 0.7 broadcast_in_dim.10
  77.2 3.9 %all-to-all-start.3 = ((bf16[32,8,256]{2,1,0:T(8,128)(2,1)}), bf16[32,8,256]{2,1,0:T(8,128)(2,1)S(1)}, u32[]{:S(2)}, u32[]{:S(2)}) async-start(bf16[32,8,256]{2,1,0:T(8,128)(2,1)} %broadcast_in_dim.10), calls=%async_computation.3 | async-start | bytes 262144 | tf_op jit(solution)/shard_map/all_to_all | solution.py:355
  81.1 0.8 copy.10
  81.9 3.1 %input_grad.1 = bf16[1024,256]{1,0:T(8,128)(2,1)} custom-call(bf16[1024,256]{1,0:T(8,128)(2,1)S(1)} %get-tuple-element.33.slope_ref, bf16[2304,256]{1,0:T(8,128)(2,1)S(1)} %get-tuple-element.26.w_ref, bf16[3,32,256]{2,1,0:T(8,128)(2,1)S(1)} %get-tuple-element.30.east_ref, bf16[3,32,256]{2,1,0:T(8,128)(2,1)S(1)} %get-tuple-element.31.west_ref, ...), custom_call_target="tpu_custom_call" | custom-call | flops 1207959552 | bytes 2097152 | tf_op jit(solution)/shard_map/input_grad/pallas_call | solution.py:375
  84.9 1.4 %factor.1 = (f32[8,144]{1,0:T(8,128)}, f32[8,144]{1,0:T(8,128)S(1)}, f32[8,128]{1,0:T(8,128)S(1)}) custom-call(f32[8,128]{1,0:T(8,128)S(1)} %slice.9.gram_ref, f32[8,144]{1,0:T(8,128)S(1)} %get-tuple-element.39.p_ref), custom_call_target="tpu_custom_call" | custom-call | tf_op jit(solution)/shard_map/factor/pallas_call | solution.py:410
  86.3 4.1 %all-to-all-done.3.s_ref = bf16[32,8,256]{2,1,0:T(8,128)(2,1)S(1)} async-done(((bf16[32,8,256]{2,1,0:T(8,128)(2,1)}), bf16[32,8,256]{2,1,0:T(8,128)(2,1)S(1)}, u32[]{:S(2)}, u32[]{:S(2)}) %all-to-all-start.3) | async-done | bytes 131104 | tf_op jit(solution)/shard_map/all_to_all | solution.py:355
  90.4 1.0 %residual.1 = (f32[144,256]{1,0:T(8,128)}, f32[8,256]{1,0:T(8,128)}) custom-call(f32[144,256]{1,0:T(8,128)S(1)} %get-tuple-element.36.matrix_ref, f32[8,144]{1,0:T(8,128)S(1)} %get-tuple-element.41.left_ref, f32[8,128]{1,0:T(8,128)S(1)} %get-tuple-element.42.solve_ref, bf16[32,8,256]{2,1,0:T(8,128)(2,1)S(1)} %all-to-all-done.3.s_ref), custom_call_target="tpu_custom_call" | custom-call | tf_op jit(solution)/shard_map/residual/pallas_call | solution.py:422
  (5 shorter events, 0.1 us)
Async XLA Ops:
  2.3 8.8 %collective-permute-start = (bf16[3,32,256]{2,1,0:T(8,128)(2,1)S(1)}, bf16[3,32,256]{2,1,0:T(8,128)(2,1)S(1)}, u32[]{:S(2)}, u32[]{:S(2)}) collective-permute-start(bf16[3,32,256]{2,1,0:T(8,128)(2,1)S(1)} %get-tuple-element.30.east_ref), channel_id=1, source_target_pairs={{0,1},{1,2},{2,3},{3,4},{4,5},{5,6},{6,7},{7,8},{8,9},{9,10},{10,1... | collective-permute-start | bytes 147464 | tf_op jit(solution)/shard_map/ppermute | solution.py:191
  5.8 5.3 %collective-permute-start.1 = (bf16[3,32,256]{2,1,0:T(8,128)(2,1)S(1)}, bf16[3,32,256]{2,1,0:T(8,128)(2,1)S(1)}, u32[]{:S(2)}, u32[]{:S(2)}) collective-permute-start(bf16[3,32,256]{2,1,0:T(8,128)(2,1)S(1)} %get-tuple-element.31.west_ref), channel_id=1, source_target_pairs={{0,15},{1,0},{2,1},{3,2},{4,3},{5,4},{6,5},{7,6},{8,7},{9,8},{10,9... | collective-permute-start | bytes 147464 | tf_op jit(solution)/shard_map/ppermute | solution.py:192
  13.6 6.6 %collective-permute-start.2 = (bf16[8,144,256]{2,1,0:T(8,128)(2,1)S(1)}, bf16[8,144,256]{2,1,0:T(8,128)(2,1)S(1)}, u32[]{:S(2)}, u32[]{:S(2)}) collective-permute-start(bf16[8,144,256]{2,1,0:T(8,128)(2,1)S(1)} %get-tuple-element.35), channel_id=1, source_target_pairs={{0,1},{1,0},{2,3},{3,2},{4,5},{5,4},{6,7},{7,6},{8,9},{9,8},{10,11... | collective-permute-start | bytes 1769480 | tf_op jit(solution)/shard_map/ppermute | solution.py:388
  20.2 23.6 %copy-start = (f32[1,144,256]{2,1,0:T(8,128)S(1)}, f32[1,144,256]{2,1,0:T(8,128)}, u32[]{:S(2)}) copy-start(f32[1,144,256]{2,1,0:T(8,128)} %param.8) | copy-start | bytes 442372
  20.2 23.6 %copy-start.1 = (f32[256,8]{0,1:T(8,128)S(1)}, f32[256,8]{0,1:T(8,128)}, u32[]{:S(2)}) copy-start(f32[256,8]{0,1:T(8,128)} %param.9) | copy-start | bytes 24580
  77.2 13.2 %all-to-all-start.3 = ((bf16[32,8,256]{2,1,0:T(8,128)(2,1)}), bf16[32,8,256]{2,1,0:T(8,128)(2,1)S(1)}, u32[]{:S(2)}, u32[]{:S(2)}) async-start(bf16[32,8,256]{2,1,0:T(8,128)(2,1)} %broadcast_in_dim.10), calls=%async_computation.3 | async-start | bytes 262144 | tf_op jit(solution)/shard_map/all_to_all | solution.py:355

commit v4 on v3

--- a/solution.py
+++ b/solution.py
@@ -221,9 +221,12 @@
 
 
 def input_grad_kernel(
-    lat, lon, slope_ref, w_ref, east_ref, west_ref, left_ref, right_ref, xgrad_ref, s_wide
+    lat, lon, out_ref, slope_ref, w_ref, east_ref, west_ref, left_ref, right_ref, out_hbm, xgrad_ref,
+    s_wide, out_sem,
 ):
     cells, ch = slope_ref.shape
+    out_copy = pltpu.make_async_copy(out_ref, out_hbm, out_sem)
+    out_copy.start()
     chunk = cells // 2
     columns = [
         shifted(left_ref[0], east_ref[1], lat),
@@ -255,6 +258,7 @@
         return carry
 
     lax.fori_loop(0, cells // chunk, input_grad, 0)
+    out_copy.wait()
 
 
 def matrix_kernel(wgrad_ref, error_ref, q_ref, matrix_ref, p_ref):
@@ -297,7 +301,7 @@
     moment_ref[:, ch : ch + 128] = parts.astype(BF16)
 
 
-def factor_kernel(gram_ref, p_ref, left_ref, held_ref, solve_ref):
+def factor_kernel(gram_ref, p_ref, left_ref, columns_ref, solve_ref):
     rank = p_ref.shape[0]
     gram = gram_ref[...]
     gram += pltpu.roll(gram, 128 - rank, 1) + pltpu.roll(gram, 128 - 2 * rank, 1)
@@ -317,11 +321,11 @@
 
         gram, p_rows, solve = step(gram), step(p_rows), step(solve)
     left_ref[...] = p_rows
-    held_ref[...] = p_rows
+    columns_ref[...] = p_rows.T
     solve_ref[...] = solve
 
 
-def residual_kernel(matrix_ref, left_ref, solve_ref, s_ref, next_ref, right_ref):
+def residual_kernel(matrix_ref, columns_ref, solve_ref, s_ref, next_ref, right_ref):
     rank = s_ref.shape[1]
     mean = image_mean(s_ref)
     solve = solve_ref[...]
@@ -329,7 +333,7 @@
     for k in range(1, rank):
         right += solve[:, k : k + 1] * mean[k : k + 1, :]
     right_ref[...] = right
-    columns = left_ref[...].T
+    columns = columns_ref[...]
     total = matrix_ref[...]
     for k in range(rank):
         total -= columns[:, k : k + 1] * right[k : k + 1, :]
@@ -372,18 +376,21 @@
     out, slope, keep, send, held = conv_call(
         x_cells, upstream_cells, kernel, lat, lon, tiles, rows_dev, scale
     )
-    xgrad = pl.pallas_call(
+    out, xgrad = pl.pallas_call(
         functools.partial(input_grad_kernel, lat, lon),
-        out_shape=sds((cells, ch), BF16),
-        in_specs=[VMEM] * 6,
-        out_specs=VMEM,
-        scratch_shapes=[pltpu.VMEM((cells + 2 * lon, 3 * ch), BF16)],
+        out_shape=(sds((cells, ch), BF16),) * 2,
+        in_specs=[VMEM] * 7,
+        out_specs=(HBM, VMEM),
+        scratch_shapes=[
+            pltpu.VMEM((cells + 2 * lon, 3 * ch), BF16),
+            pltpu.SemaphoreType.DMA,
+        ],
         compiler_params=pltpu.CompilerParams(vmem_limit_bytes=BIG),
         cost_estimate=pl.CostEstimate(
             flops=2 * cells * kernel_rows * ch, bytes_accessed=2 * 2**20, transcendentals=0
         ),
         name="input_grad",
-    )(slope, *held)
+    )(out, slope, *held)
 
     summed = keep + lax.ppermute(send, "tile", cores("tile"))
     wgrad_rows = lax.all_to_all(
@@ -407,11 +414,11 @@
         name="moment",
     )(matrix, shares_of(p_local, "dp"))
     moment = shares_of(moment, "tile").astype(F32).sum(0)
-    p_factor, held_factor, solve = pl.pallas_call(
+    p_factor, columns, solve = pl.pallas_call(
         factor_kernel,
         out_shape=(
             sds((rank, rows_dev), F32),
-            local((rank, rows_dev), F32),
+            local((rows_dev, rank), F32),
             local((rank, 128), F32),
         ),
         in_specs=[VMEM] * 2,
@@ -426,7 +433,7 @@
         out_specs=(VMEM,) * 2,
         compiler_params=small,
         name="residual",
-    )(matrix, held_factor, solve, shares_of(moment[:, :ch].astype(BF16), "dp"))
+    )(matrix, columns, solve, shares_of(moment[:, :ch].astype(BF16), "dp"))
 
     shape = inputs.shape
     return (out.reshape(shape), xgrad.reshape(shape), p_factor.T, q_factor.T, new_feedback[None])

time: 91.8 us -> 91.7 us (level)
  transfers between devices with their start and end apart: 4 -> 4, of which waited for: 2 -> 2; matrix products, arithmetic and copies ran while one was open for 1% -> 0% of each run, Pallas kernels for 7% -> 7%
where the time goes in v4:
time: 91.7 us; the launch traced here: 91.3 us
  blocking collectives  55.6 us (61%)
  starting transfers between devices  15.8 us (17%)
  Pallas kernels  11.8 us (13%)
  waiting for transfers between devices  6.5 us (7%)
    all_to_all x2, blocking collectives, shares_of(): lax.all_to_all(jnp.broadcast_to(value[None], (count,) + value.shape), axi...  32.1 us
    all_to_all x1, blocking collectives, per_device(): lax.all_to_all(summed, 'tile', 0, 0, axis_index_groups=chips('tile'), til...  23.5 us
    ppermute x1, starting transfers between devices, per_device(): summed = keep + lax.ppermute(send, 'tile', cores('tile'))  5.03 us
    all_to_all x1, waiting for transfers between devices, shares_of(): lax.all_to_all(jnp.broadcast_to(value[None], (count,) + value.shape), axi...  4.89 us
    all_to_all x1, starting transfers between devices, shares_of(): lax.all_to_all(jnp.broadcast_to(value[None], (count,) + value.shape), axi...  3.86 us
    ppermute x1, starting transfers between devices, conv_call(): left = lax.ppermute(east, 'tile', shift('tile', 1))  3.49 us
    ppermute x1, starting transfers between devices, conv_call(): right = lax.ppermute(west, 'tile', shift('tile', -1))  3.42 us
    pallas_call x1, Pallas kernels, per_device(): pl.pallas_call(functools.partial(input_grad_kernel, lat, lon), out_shape=...  3.09 us
  transfers between devices with their start and end apart: 4, of which 2 were waited for; matrix products, arithmetic and copies ran while one was open for 0% of the time, Pallas kernels for 7%

profile of v4, /device:TPU:1, one launch (start us, length us, event | category | flops | bytes accessed | tf_op | source)
XLA Modules:
  0.0 91.3 jit_solution(7581580178497283667)
XLA Ops:
  0.6 1.6 %load.1 = (bf16[1024,256]{1,0:T(8,128)(2,1)S(1)}, bf16[1024,256]{1,0:T(8,128)(2,1)S(1)}, bf16[2304,256]{1,0:T(8,128)(2,1)S(1)}, bf16[3,32,256]{2,1,0:T(8,128)(2,1)S(1)}, bf16[3,32,256]{2,1,0:T(8,128)(2,1)S(1)}) custom-call(bf16[1024,256]{1,0:T(8,128)(2,1)} %bitcast.11, bf16[1024,256]{1,0:T(8,128)(2,1)} %bitcast.12, bf16[2304,256]{1,0:T(8,128)(2,1)} %w_hbm.1), custom_call_target="tpu_custom_call" | custom-call | tf_op jit(solution)/shard_map/load/pallas_call | solution.py:182
  2.3 3.5 %collective-permute-start = (bf16[3,32,256]{2,1,0:T(8,128)(2,1)S(1)}, bf16[3,32,256]{2,1,0:T(8,128)(2,1)S(1)}, u32[]{:S(2)}, u32[]{:S(2)}) collective-permute-start(bf16[3,32,256]{2,1,0:T(8,128)(2,1)S(1)} %get-tuple-element.32.east_ref), channel_id=1, source_target_pairs={{0,1},{1,2},{2,3},{3,4},{4,5},{5,6},{6,7},{7,8},{8,9},{9,10},{10,1... | collective-permute-start | bytes 147464 | tf_op jit(solution)/shard_map/ppermute | solution.py:191
  5.8 3.4 %collective-permute-start.1 = (bf16[3,32,256]{2,1,0:T(8,128)(2,1)S(1)}, bf16[3,32,256]{2,1,0:T(8,128)(2,1)S(1)}, u32[]{:S(2)}, u32[]{:S(2)}) collective-permute-start(bf16[3,32,256]{2,1,0:T(8,128)(2,1)S(1)} %get-tuple-element.33.west_ref), channel_id=1, source_target_pairs={{0,15},{1,0},{2,1},{3,2},{4,3},{5,4},{6,5},{7,6},{8,7},{9,8},{10,9... | collective-permute-start | bytes 147464 | tf_op jit(solution)/shard_map/ppermute | solution.py:192
  9.2 1.8 %inner.1 = (bf16[1088,768]{1,0:T(8,128)(2,1)S(1)}, f32[1024,256]{1,0:T(8,128)S(1)}) custom-call(bf16[1024,256]{1,0:T(8,128)(2,1)S(1)} %get-tuple-element.27.x_ref, bf16[2304,256]{1,0:T(8,128)(2,1)S(1)} %get-tuple-element.28.w_ref), custom_call_target="tpu_custom_call" | custom-call | flops 1207959552 | tf_op jit(solution)/shard_map/inner/pallas_call | solution.py:193
  11.0 0.0 collective-permute-done.left_ref
  11.0 0.0 collective-permute-done.1.right_ref
  11.0 2.5 %conv.1 = (bf16[1024,256]{1,0:T(8,128)(2,1)S(1)}, bf16[1024,256]{1,0:T(8,128)(2,1)S(1)}, bf16[8,144,256]{2,1,0:T(8,128)(2,1)S(1)}, bf16[8,144,256]{2,1,0:T(8,128)(2,1)S(1)}) custom-call(bf16[1088,768]{1,0:T(8,128)(2,1)S(1)} %get-tuple-element.29.x_wide, f32[1024,256]{1,0:T(8,128)S(1)} %get-tuple-element.30.preact_ref, ...), custom_call_target="tpu_custom_call" | custom-call | flops 1207959552 | bytes 1048576 | tf_op jit(solution)/shard_map/conv/pallas_call | solution.py:205
  13.6 5.0 %collective-permute-start.2 = (bf16[8,144,256]{2,1,0:T(8,128)(2,1)S(1)}, bf16[8,144,256]{2,1,0:T(8,128)(2,1)S(1)}, u32[]{:S(2)}, u32[]{:S(2)}) collective-permute-start(bf16[8,144,256]{2,1,0:T(8,128)(2,1)S(1)} %get-tuple-element.39), channel_id=1, source_target_pairs={{0,1},{1,0},{2,3},{3,2},{4,5},{5,4},{6,7},{7,6},{8,9},{9,8},{10,11... | collective-permute-start | bytes 1769480 | tf_op jit(solution)/shard_map/ppermute | solution.py:395
  18.6 1.6 %collective-permute-done.2 = bf16[8,144,256]{2,1,0:T(8,128)(2,1)S(1)} collective-permute-done((bf16[8,144,256]{2,1,0:T(8,128)(2,1)S(1)}, bf16[8,144,256]{2,1,0:T(8,128)(2,1)S(1)}, u32[]{:S(2)}, u32[]{:S(2)}) %collective-permute-start.2) | collective-permute-done | bytes 589856 | tf_op jit(solution)/shard_map/ppermute | solution.py:395
  20.2 0.0 copy-start
  20.2 0.0 copy-start.1
  20.2 0.1 add.3
  20.4 23.5 %all_to_all.20.wgrad_ref = bf16[8,144,256]{2,1,0:T(8,128)(2,1)S(1)} all-to-all(bf16[8,144,256]{2,1,0:T(8,128)(2,1)S(1)} %add.3), channel_id=1, replica_groups={{0,2,4,6,8,10,12,14},{1,3,5,7,9,11,13,15},{16,18,20,22,24,26,28,30},{17..., dimensions={0} | all-to-all | bytes 1179648 | tf_op jit(solution)/shard_map/all_to_all | solution.py:396
  43.8 0.0 copy-done
  43.8 0.0 copy-done.1
  43.8 0.2 matrix.1
  44.1 18.6 %all_to_all.21.p_ref = bf16[32,8,144]{2,1,0:T(8,128)(2,1)S(1)} all-to-all(bf16[32,8,144]{2,1,0:T(8,128)(2,1)S(1)} %broadcast_in_dim.8), channel_id=1, replica_groups=mesh['dp'=32,'tile'=16] {'dp'}, dimensions={0} | all-to-all | bytes 147456 | tf_op jit(solution)/shard_map/all_to_all | solution.py:359
  62.7 0.2 moment.1
  63.0 13.5 %all_to_all.22 = bf16[16,8,384]{2,1,0:T(8,128)(2,1)S(1)} all-to-all(bf16[16,8,384]{2,1,0:T(8,128)(2,1)S(1)} %broadcast_in_dim.9), channel_id=1, replica_groups=mesh['dp'=32,'tile'=16] {'tile'}, dimensions={0} | all-to-all | bytes 196608 | tf_op jit(solution)/shard_map/all_to_all | solution.py:359
  76.5 0.7 broadcast_in_dim.10
  77.2 3.9 %all-to-all-start.3 = ((bf16[32,8,256]{2,1,0:T(8,128)(2,1)}), bf16[32,8,256]{2,1,0:T(8,128)(2,1)S(1)}, u32[]{:S(2)}, u32[]{:S(2)}) async-start(bf16[32,8,256]{2,1,0:T(8,128)(2,1)} %broadcast_in_dim.10), calls=%async_computation.3 | async-start | bytes 262144 | tf_op jit(solution)/shard_map/all_to_all | solution.py:359
  81.0 3.1 %input_grad.1 = (bf16[1024,256]{1,0:T(8,128)(2,1)}, bf16[1024,256]{1,0:T(8,128)(2,1)}) custom-call(bf16[1024,256]{1,0:T(8,128)(2,1)S(1)} %get-tuple-element.34.out_ref, bf16[1024,256]{1,0:T(8,128)(2,1)S(1)} %get-tuple-element.35.slope_ref, bf16[2304,256]{1,0:T(8,128)(2,1)S(1)} %get-tuple-element.28.w_ref, ...), custom_call_target="tpu_custom_call" | custom-call | flops 1207959552 | bytes 2097152 | tf_op jit(solution)/shard_map/input_grad/pallas_call | solution.py:379
  84.2 1.4 %factor.1 = (f32[8,144]{1,0:T(8,128)}, f32[144,8]{1,0:T(8,128)S(1)}, f32[8,128]{1,0:T(8,128)S(1)}) custom-call(f32[8,128]{1,0:T(8,128)S(1)} %slice.9.gram_ref, f32[8,144]{1,0:T(8,128)S(1)} %get-tuple-element.43.p_ref), custom_call_target="tpu_custom_call" | custom-call | tf_op jit(solution)/shard_map/factor/pallas_call | solution.py:417
  85.5 4.9 %all-to-all-done.3.s_ref = bf16[32,8,256]{2,1,0:T(8,128)(2,1)S(1)} async-done(((bf16[32,8,256]{2,1,0:T(8,128)(2,1)}), bf16[32,8,256]{2,1,0:T(8,128)(2,1)S(1)}, u32[]{:S(2)}, u32[]{:S(2)}) %all-to-all-start.3) | async-done | bytes 131104 | tf_op jit(solution)/shard_map/all_to_all | solution.py:359
  90.4 0.9 %residual.1 = (f32[144,256]{1,0:T(8,128)}, f32[8,256]{1,0:T(8,128)}) custom-call(f32[144,256]{1,0:T(8,128)S(1)} %get-tuple-element.40.matrix_ref, f32[144,8]{1,0:T(8,128)S(1)} %get-tuple-element.45.columns_ref, f32[8,128]{1,0:T(8,128)S(1)} %get-tuple-element.46.solve_ref, bf16[32,8,256]{2,1,0:T(8,128)(2,1)S(1)} %all-to-all-done.3.s_ref), custom_call_target="tpu_custom_call" | custom-call | tf_op jit(solution)/shard_map/residual/pallas_call | solution.py:429
  (5 shorter events, 0.1 us)
Async XLA Ops:
  2.3 8.8 %collective-permute-start = (bf16[3,32,256]{2,1,0:T(8,128)(2,1)S(1)}, bf16[3,32,256]{2,1,0:T(8,128)(2,1)S(1)}, u32[]{:S(2)}, u32[]{:S(2)}) collective-permute-start(bf16[3,32,256]{2,1,0:T(8,128)(2,1)S(1)} %get-tuple-element.32.east_ref), channel_id=1, source_target_pairs={{0,1},{1,2},{2,3},{3,4},{4,5},{5,6},{6,7},{7,8},{8,9},{9,10},{10,1... | collective-permute-start | bytes 147464 | tf_op jit(solution)/shard_map/ppermute | solution.py:191
  5.8 5.3 %collective-permute-start.1 = (bf16[3,32,256]{2,1,0:T(8,128)(2,1)S(1)}, bf16[3,32,256]{2,1,0:T(8,128)(2,1)S(1)}, u32[]{:S(2)}, u32[]{:S(2)}) collective-permute-start(bf16[3,32,256]{2,1,0:T(8,128)(2,1)S(1)} %get-tuple-element.33.west_ref), channel_id=1, source_target_pairs={{0,15},{1,0},{2,1},{3,2},{4,3},{5,4},{6,5},{7,6},{8,7},{9,8},{10,9... | collective-permute-start | bytes 147464 | tf_op jit(solution)/shard_map/ppermute | solution.py:192
  13.6 6.6 %collective-permute-start.2 = (bf16[8,144,256]{2,1,0:T(8,128)(2,1)S(1)}, bf16[8,144,256]{2,1,0:T(8,128)(2,1)S(1)}, u32[]{:S(2)}, u32[]{:S(2)}) collective-permute-start(bf16[8,144,256]{2,1,0:T(8,128)(2,1)S(1)} %get-tuple-element.39), channel_id=1, source_target_pairs={{0,1},{1,0},{2,3},{3,2},{4,5},{5,4},{6,7},{7,6},{8,9},{9,8},{10,11... | collective-permute-start | bytes 1769480 | tf_op jit(solution)/shard_map/ppermute | solution.py:395
  20.2 23.6 %copy-start = (f32[1,144,256]{2,1,0:T(8,128)S(1)}, f32[1,144,256]{2,1,0:T(8,128)}, u32[]{:S(2)}) copy-start(f32[1,144,256]{2,1,0:T(8,128)} %param.8) | copy-start | bytes 442372
  20.2 23.6 %copy-start.1 = (f32[256,8]{0,1:T(8,128)S(1)}, f32[256,8]{0,1:T(8,128)}, u32[]{:S(2)}) copy-start(f32[256,8]{0,1:T(8,128)} %param.9) | copy-start | bytes 24580
  77.2 13.2 %all-to-all-start.3 = ((bf16[32,8,256]{2,1,0:T(8,128)(2,1)}), bf16[32,8,256]{2,1,0:T(8,128)(2,1)S(1)}, u32[]{:S(2)}, u32[]{:S(2)}) async-start(bf16[32,8,256]{2,1,0:T(8,128)(2,1)} %broadcast_in_dim.10), calls=%async_computation.3 | async-start | bytes 262144 | tf_op jit(solution)/shard_map/all_to_all | solution.py:359

commit v5 on v4

--- a/solution.py
+++ b/solution.py
@@ -167,10 +167,15 @@
         )
         wgrad_ref[k * ch : (k + 1) * ch, :] = (term * scale).astype(BF16)
     pairs, piece, _ = keep_ref.shape
-    for pair in range(pairs):
-        for held, owner in ((keep_ref, core), (send_ref, 1 - core)):
-            start = pl.multiple_of((2 * pair + owner) * piece, 16)
-            held[pair] = wgrad_ref[pl.ds(start, piece), :]
+
+    def divide(own):
+        for pair in range(pairs):
+            for held, owner in ((keep_ref, own), (send_ref, 1 - own)):
+                start = (2 * pair + owner) * piece
+                held[pair] = wgrad_ref[start : start + piece, :]
+
+    for own in range(2):
+        pl.when(core == own)(functools.partial(divide, own))
 
 
 def conv_call(x, upstream, kernel, lat, lon, tiles, rows_dev, scale):

time: 91.7 us -> 91.3 us (level)
  no operation moved by 1% of the time
where the time goes in v5:
time: 91.3 us; the launch traced here: 91 us
  blocking collectives  55.6 us (61%)
  starting transfers between devices  15.8 us (17%)
  Pallas kernels  11.5 us (13%)
  waiting for transfers between devices  6.5 us (7%)
    all_to_all x2, blocking collectives, shares_of(): lax.all_to_all(jnp.broadcast_to(value[None], (count,) + value.shape), axi...  32.1 us
    all_to_all x1, blocking collectives, per_device(): lax.all_to_all(summed, 'tile', 0, 0, axis_index_groups=chips('tile'), til...  23.5 us
    ppermute x1, starting transfers between devices, per_device(): summed = keep + lax.ppermute(send, 'tile', cores('tile'))  5.01 us
    all_to_all x1, waiting for transfers between devices, shares_of(): lax.all_to_all(jnp.broadcast_to(value[None], (count,) + value.shape), axi...  4.89 us
    all_to_all x1, starting transfers between devices, shares_of(): lax.all_to_all(jnp.broadcast_to(value[None], (count,) + value.shape), axi...  3.86 us
    ppermute x1, starting transfers between devices, conv_call(): left = lax.ppermute(east, 'tile', shift('tile', 1))  3.49 us
    ppermute x1, starting transfers between devices, conv_call(): right = lax.ppermute(west, 'tile', shift('tile', -1))  3.42 us
    pallas_call x1, Pallas kernels, per_device(): pl.pallas_call(functools.partial(input_grad_kernel, lat, lon), out_shape=...  3.09 us
  transfers between devices with their start and end apart: 4, of which 2 were waited for; matrix products, arithmetic and copies ran while one was open for 0% of the time, Pallas kernels for 7%

profile of v5, /device:TPU:1, one launch (start us, length us, event | category | flops | bytes accessed | tf_op | source)
XLA Modules:
  0.0 91.0 jit_solution(15607356849419157102)
XLA Ops:
  0.6 1.6 %load.1 = (bf16[1024,256]{1,0:T(8,128)(2,1)S(1)}, bf16[1024,256]{1,0:T(8,128)(2,1)S(1)}, bf16[2304,256]{1,0:T(8,128)(2,1)S(1)}, bf16[3,32,256]{2,1,0:T(8,128)(2,1)S(1)}, bf16[3,32,256]{2,1,0:T(8,128)(2,1)S(1)}) custom-call(bf16[1024,256]{1,0:T(8,128)(2,1)} %bitcast.11, bf16[1024,256]{1,0:T(8,128)(2,1)} %bitcast.12, bf16[2304,256]{1,0:T(8,128)(2,1)} %w_hbm.1), custom_call_target="tpu_custom_call" | custom-call | tf_op jit(solution)/shard_map/load/pallas_call | solution.py:187
  2.3 3.5 %collective-permute-start = (bf16[3,32,256]{2,1,0:T(8,128)(2,1)S(1)}, bf16[3,32,256]{2,1,0:T(8,128)(2,1)S(1)}, u32[]{:S(2)}, u32[]{:S(2)}) collective-permute-start(bf16[3,32,256]{2,1,0:T(8,128)(2,1)S(1)} %get-tuple-element.32.east_ref), channel_id=1, source_target_pairs={{0,1},{1,2},{2,3},{3,4},{4,5},{5,6},{6,7},{7,8},{8,9},{9,10},{10,1... | collective-permute-start | bytes 147464 | tf_op jit(solution)/shard_map/ppermute | solution.py:196
  5.8 3.4 %collective-permute-start.1 = (bf16[3,32,256]{2,1,0:T(8,128)(2,1)S(1)}, bf16[3,32,256]{2,1,0:T(8,128)(2,1)S(1)}, u32[]{:S(2)}, u32[]{:S(2)}) collective-permute-start(bf16[3,32,256]{2,1,0:T(8,128)(2,1)S(1)} %get-tuple-element.33.west_ref), channel_id=1, source_target_pairs={{0,15},{1,0},{2,1},{3,2},{4,3},{5,4},{6,5},{7,6},{8,7},{9,8},{10,9... | collective-permute-start | bytes 147464 | tf_op jit(solution)/shard_map/ppermute | solution.py:197
  9.2 1.8 %inner.1 = (bf16[1088,768]{1,0:T(8,128)(2,1)S(1)}, f32[1024,256]{1,0:T(8,128)S(1)}) custom-call(bf16[1024,256]{1,0:T(8,128)(2,1)S(1)} %get-tuple-element.27.x_ref, bf16[2304,256]{1,0:T(8,128)(2,1)S(1)} %get-tuple-element.28.w_ref), custom_call_target="tpu_custom_call" | custom-call | flops 1207959552 | tf_op jit(solution)/shard_map/inner/pallas_call | solution.py:198
  11.0 0.0 collective-permute-done.left_ref
  11.0 0.0 collective-permute-done.1.right_ref
  11.0 2.2 %conv.1 = (bf16[1024,256]{1,0:T(8,128)(2,1)S(1)}, bf16[1024,256]{1,0:T(8,128)(2,1)S(1)}, bf16[8,144,256]{2,1,0:T(8,128)(2,1)S(1)}, bf16[8,144,256]{2,1,0:T(8,128)(2,1)S(1)}) custom-call(bf16[1088,768]{1,0:T(8,128)(2,1)S(1)} %get-tuple-element.29.x_wide, f32[1024,256]{1,0:T(8,128)S(1)} %get-tuple-element.30.preact_ref, ...), custom_call_target="tpu_custom_call" | custom-call | flops 1207959552 | bytes 1048576 | tf_op jit(solution)/shard_map/conv/pallas_call | solution.py:210
  13.2 5.0 %collective-permute-start.2 = (bf16[8,144,256]{2,1,0:T(8,128)(2,1)S(1)}, bf16[8,144,256]{2,1,0:T(8,128)(2,1)S(1)}, u32[]{:S(2)}, u32[]{:S(2)}) collective-permute-start(bf16[8,144,256]{2,1,0:T(8,128)(2,1)S(1)} %get-tuple-element.39), channel_id=1, source_target_pairs={{0,1},{1,0},{2,3},{3,2},{4,5},{5,4},{6,7},{7,6},{8,9},{9,8},{10,11... | collective-permute-start | bytes 1769480 | tf_op jit(solution)/shard_map/ppermute | solution.py:400
  18.2 1.6 %collective-permute-done.2 = bf16[8,144,256]{2,1,0:T(8,128)(2,1)S(1)} collective-permute-done((bf16[8,144,256]{2,1,0:T(8,128)(2,1)S(1)}, bf16[8,144,256]{2,1,0:T(8,128)(2,1)S(1)}, u32[]{:S(2)}, u32[]{:S(2)}) %collective-permute-start.2) | collective-permute-done | bytes 589856 | tf_op jit(solution)/shard_map/ppermute | solution.py:400
  19.9 0.0 copy-start
  19.9 0.0 copy-start.1
  19.9 0.1 add.3
  20.0 23.5 %all_to_all.20.wgrad_ref = bf16[8,144,256]{2,1,0:T(8,128)(2,1)S(1)} all-to-all(bf16[8,144,256]{2,1,0:T(8,128)(2,1)S(1)} %add.3), channel_id=1, replica_groups={{0,2,4,6,8,10,12,14},{1,3,5,7,9,11,13,15},{16,18,20,22,24,26,28,30},{17..., dimensions={0} | all-to-all | bytes 1179648 | tf_op jit(solution)/shard_map/all_to_all | solution.py:401
  43.5 0.0 copy-done
  43.5 0.0 copy-done.1
  43.5 0.2 matrix.1
  43.8 18.6 %all_to_all.21.p_ref = bf16[32,8,144]{2,1,0:T(8,128)(2,1)S(1)} all-to-all(bf16[32,8,144]{2,1,0:T(8,128)(2,1)S(1)} %broadcast_in_dim.8), channel_id=1, replica_groups=mesh['dp'=32,'tile'=16] {'dp'}, dimensions={0} | all-to-all | bytes 147456 | tf_op jit(solution)/shard_map/all_to_all | solution.py:364
  62.4 0.2 moment.1
  62.6 13.5 %all_to_all.22 = bf16[16,8,384]{2,1,0:T(8,128)(2,1)S(1)} all-to-all(bf16[16,8,384]{2,1,0:T(8,128)(2,1)S(1)} %broadcast_in_dim.9), channel_id=1, replica_groups=mesh['dp'=32,'tile'=16] {'tile'}, dimensions={0} | all-to-all | bytes 196608 | tf_op jit(solution)/shard_map/all_to_all | solution.py:364
  76.2 0.7 broadcast_in_dim.10
  76.8 3.9 %all-to-all-start.3 = ((bf16[32,8,256]{2,1,0:T(8,128)(2,1)}), bf16[32,8,256]{2,1,0:T(8,128)(2,1)S(1)}, u32[]{:S(2)}, u32[]{:S(2)}) async-start(bf16[32,8,256]{2,1,0:T(8,128)(2,1)} %broadcast_in_dim.10), calls=%async_computation.3 | async-start | bytes 262144 | tf_op jit(solution)/shard_map/all_to_all | solution.py:364
  80.7 3.1 %input_grad.1 = (bf16[1024,256]{1,0:T(8,128)(2,1)}, bf16[1024,256]{1,0:T(8,128)(2,1)}) custom-call(bf16[1024,256]{1,0:T(8,128)(2,1)S(1)} %get-tuple-element.34.out_ref, bf16[1024,256]{1,0:T(8,128)(2,1)S(1)} %get-tuple-element.35.slope_ref, bf16[2304,256]{1,0:T(8,128)(2,1)S(1)} %get-tuple-element.28.w_ref, ...), custom_call_target="tpu_custom_call" | custom-call | flops 1207959552 | bytes 2097152 | tf_op jit(solution)/shard_map/input_grad/pallas_call | solution.py:384
  83.8 1.4 %factor.1 = (f32[8,144]{1,0:T(8,128)}, f32[144,8]{1,0:T(8,128)S(1)}, f32[8,128]{1,0:T(8,128)S(1)}) custom-call(f32[8,128]{1,0:T(8,128)S(1)} %slice.9.gram_ref, f32[8,144]{1,0:T(8,128)S(1)} %get-tuple-element.43.p_ref), custom_call_target="tpu_custom_call" | custom-call | tf_op jit(solution)/shard_map/factor/pallas_call | solution.py:422
  85.2 4.9 %all-to-all-done.3.s_ref = bf16[32,8,256]{2,1,0:T(8,128)(2,1)S(1)} async-done(((bf16[32,8,256]{2,1,0:T(8,128)(2,1)}), bf16[32,8,256]{2,1,0:T(8,128)(2,1)S(1)}, u32[]{:S(2)}, u32[]{:S(2)}) %all-to-all-start.3) | async-done | bytes 131104 | tf_op jit(solution)/shard_map/all_to_all | solution.py:364
  90.1 0.9 %residual.1 = (f32[144,256]{1,0:T(8,128)}, f32[8,256]{1,0:T(8,128)}) custom-call(f32[144,256]{1,0:T(8,128)S(1)} %get-tuple-element.40.matrix_ref, f32[144,8]{1,0:T(8,128)S(1)} %get-tuple-element.45.columns_ref, f32[8,128]{1,0:T(8,128)S(1)} %get-tuple-element.46.solve_ref, bf16[32,8,256]{2,1,0:T(8,128)(2,1)S(1)} %all-to-all-done.3.s_ref), custom_call_target="tpu_custom_call" | custom-call | tf_op jit(solution)/shard_map/residual/pallas_call | solution.py:434
  (5 shorter events, 0.1 us)
Async XLA Ops:
  2.3 8.8 %collective-permute-start = (bf16[3,32,256]{2,1,0:T(8,128)(2,1)S(1)}, bf16[3,32,256]{2,1,0:T(8,128)(2,1)S(1)}, u32[]{:S(2)}, u32[]{:S(2)}) collective-permute-start(bf16[3,32,256]{2,1,0:T(8,128)(2,1)S(1)} %get-tuple-element.32.east_ref), channel_id=1, source_target_pairs={{0,1},{1,2},{2,3},{3,4},{4,5},{5,6},{6,7},{7,8},{8,9},{9,10},{10,1... | collective-permute-start | bytes 147464 | tf_op jit(solution)/shard_map/ppermute | solution.py:196
  5.8 5.3 %collective-permute-start.1 = (bf16[3,32,256]{2,1,0:T(8,128)(2,1)S(1)}, bf16[3,32,256]{2,1,0:T(8,128)(2,1)S(1)}, u32[]{:S(2)}, u32[]{:S(2)}) collective-permute-start(bf16[3,32,256]{2,1,0:T(8,128)(2,1)S(1)} %get-tuple-element.33.west_ref), channel_id=1, source_target_pairs={{0,15},{1,0},{2,1},{3,2},{4,3},{5,4},{6,5},{7,6},{8,7},{9,8},{10,9... | collective-permute-start | bytes 147464 | tf_op jit(solution)/shard_map/ppermute | solution.py:197
  13.2 6.6 %collective-permute-start.2 = (bf16[8,144,256]{2,1,0:T(8,128)(2,1)S(1)}, bf16[8,144,256]{2,1,0:T(8,128)(2,1)S(1)}, u32[]{:S(2)}, u32[]{:S(2)}) collective-permute-start(bf16[8,144,256]{2,1,0:T(8,128)(2,1)S(1)} %get-tuple-element.39), channel_id=1, source_target_pairs={{0,1},{1,0},{2,3},{3,2},{4,5},{5,4},{6,7},{7,6},{8,9},{9,8},{10,11... | collective-permute-start | bytes 1769480 | tf_op jit(solution)/shard_map/ppermute | solution.py:400
  19.9 23.6 %copy-start = (f32[1,144,256]{2,1,0:T(8,128)S(1)}, f32[1,144,256]{2,1,0:T(8,128)}, u32[]{:S(2)}) copy-start(f32[1,144,256]{2,1,0:T(8,128)} %param.8) | copy-start | bytes 442372
  19.9 23.6 %copy-start.1 = (f32[256,8]{0,1:T(8,128)S(1)}, f32[256,8]{0,1:T(8,128)}, u32[]{:S(2)}) copy-start(f32[256,8]{0,1:T(8,128)} %param.9) | copy-start | bytes 24580
  76.8 13.2 %all-to-all-start.3 = ((bf16[32,8,256]{2,1,0:T(8,128)(2,1)}), bf16[32,8,256]{2,1,0:T(8,128)(2,1)S(1)}, u32[]{:S(2)}, u32[]{:S(2)}) async-start(bf16[32,8,256]{2,1,0:T(8,128)(2,1)} %broadcast_in_dim.10), calls=%async_computation.3 | async-start | bytes 262144 | tf_op jit(solution)/shard_map/all_to_all | solution.py:364

commit v6 on v5

--- a/solution.py
+++ b/solution.py
@@ -169,10 +169,10 @@
     pairs, piece, _ = keep_ref.shape
 
     def divide(own):
-        for pair in range(pairs):
+        for place, chip in enumerate(ring_order(pairs)):
             for held, owner in ((keep_ref, own), (send_ref, 1 - own)):
-                start = (2 * pair + owner) * piece
-                held[pair] = wgrad_ref[start : start + piece, :]
+                start = (2 * chip + owner) * piece
+                held[place] = wgrad_ref[start : start + piece, :]
 
     for own in range(2):
         pl.when(core == own)(functools.partial(divide, own))
@@ -354,9 +354,17 @@
     return [(i, i ^ 1) for i in range(lax.axis_size(axis))]
 
 
+def ring_order(count):
+    order, step = [0], count
+    while len(order) < count:
+        step //= 2
+        order += [chip + step for chip in order]
+    return order
+
+
 def chips(axis):
-    count = lax.axis_size(axis)
-    return [list(range(core, count, 2)) for core in range(2)]
+    order = ring_order(lax.axis_size(axis) // 2)
+    return [[2 * chip + core for chip in order] for core in range(2)]
 
 
 def shares_of(value, axis):

time: 91.3 us -> 90.6 us (level)
    all_to_all x1, blocking collectives: 23.5 us -> 21.8 us  [per_device(): lax.all_to_all(summed, 'tile', 0, 0, axis_index_groups=chips('tile'), til...]
    all_to_all x2, blocking collectives: 32.1 us -> 33.1 us  [shares_of(): lax.all_to_all(jnp.broadcast_to(value[None], (count,) + value.shape), axi...]
where the time goes in v6:
time: 90.6 us; the launch traced here: 90.3 us
  blocking collectives  54.9 us (61%)
  starting transfers between devices  15.8 us (17%)
  Pallas kernels  11.5 us (13%)
  waiting for transfers between devices  6.5 us (7%)
    all_to_all x2, blocking collectives, shares_of(): lax.all_to_all(jnp.broadcast_to(value[None], (count,) + value.shape), axi...  33.1 us
    all_to_all x1, blocking collectives, per_device(): lax.all_to_all(summed, 'tile', 0, 0, axis_index_groups=chips('tile'), til...  21.8 us
    ppermute x1, starting transfers between devices, per_device(): summed = keep + lax.ppermute(send, 'tile', cores('tile'))  5.01 us
    all_to_all x1, waiting for transfers between devices, shares_of(): lax.all_to_all(jnp.broadcast_to(value[None], (count,) + value.shape), axi...  4.89 us
    all_to_all x1, starting transfers between devices, shares_of(): lax.all_to_all(jnp.broadcast_to(value[None], (count,) + value.shape), axi...  3.86 us
    ppermute x1, starting transfers between devices, conv_call(): left = lax.ppermute(east, 'tile', shift('tile', 1))  3.49 us
    ppermute x1, starting transfers between devices, conv_call(): right = lax.ppermute(west, 'tile', shift('tile', -1))  3.42 us
    pallas_call x1, Pallas kernels, per_device(): pl.pallas_call(functools.partial(input_grad_kernel, lat, lon), out_shape=...  3.09 us
  transfers between devices with their start and end apart: 4, of which 2 were waited for; matrix products, arithmetic and copies ran while one was open for 0% of the time, Pallas kernels for 7%

profile of v6, /device:TPU:1, one launch (start us, length us, event | category | flops | bytes accessed | tf_op | source)
XLA Modules:
  0.0 90.3 jit_solution(10641061299015583698)
XLA Ops:
  0.6 1.6 %load.1 = (bf16[1024,256]{1,0:T(8,128)(2,1)S(1)}, bf16[1024,256]{1,0:T(8,128)(2,1)S(1)}, bf16[2304,256]{1,0:T(8,128)(2,1)S(1)}, bf16[3,32,256]{2,1,0:T(8,128)(2,1)S(1)}, bf16[3,32,256]{2,1,0:T(8,128)(2,1)S(1)}) custom-call(bf16[1024,256]{1,0:T(8,128)(2,1)} %bitcast.11, bf16[1024,256]{1,0:T(8,128)(2,1)} %bitcast.12, bf16[2304,256]{1,0:T(8,128)(2,1)} %w_hbm.1), custom_call_target="tpu_custom_call" | custom-call | tf_op jit(solution)/shard_map/load/pallas_call | solution.py:187
  2.3 3.5 %collective-permute-start = (bf16[3,32,256]{2,1,0:T(8,128)(2,1)S(1)}, bf16[3,32,256]{2,1,0:T(8,128)(2,1)S(1)}, u32[]{:S(2)}, u32[]{:S(2)}) collective-permute-start(bf16[3,32,256]{2,1,0:T(8,128)(2,1)S(1)} %get-tuple-element.32.east_ref), channel_id=1, source_target_pairs={{0,1},{1,2},{2,3},{3,4},{4,5},{5,6},{6,7},{7,8},{8,9},{9,10},{10,1... | collective-permute-start | bytes 147464 | tf_op jit(solution)/shard_map/ppermute | solution.py:196
  5.8 3.4 %collective-permute-start.1 = (bf16[3,32,256]{2,1,0:T(8,128)(2,1)S(1)}, bf16[3,32,256]{2,1,0:T(8,128)(2,1)S(1)}, u32[]{:S(2)}, u32[]{:S(2)}) collective-permute-start(bf16[3,32,256]{2,1,0:T(8,128)(2,1)S(1)} %get-tuple-element.33.west_ref), channel_id=1, source_target_pairs={{0,15},{1,0},{2,1},{3,2},{4,3},{5,4},{6,5},{7,6},{8,7},{9,8},{10,9... | collective-permute-start | bytes 147464 | tf_op jit(solution)/shard_map/ppermute | solution.py:197
  9.2 1.8 %inner.1 = (bf16[1088,768]{1,0:T(8,128)(2,1)S(1)}, f32[1024,256]{1,0:T(8,128)S(1)}) custom-call(bf16[1024,256]{1,0:T(8,128)(2,1)S(1)} %get-tuple-element.27.x_ref, bf16[2304,256]{1,0:T(8,128)(2,1)S(1)} %get-tuple-element.28.w_ref), custom_call_target="tpu_custom_call" | custom-call | flops 1207959552 | tf_op jit(solution)/shard_map/inner/pallas_call | solution.py:198
  11.0 0.0 collective-permute-done.left_ref
  11.0 0.0 collective-permute-done.1.right_ref
  11.0 2.2 %conv.1 = (bf16[1024,256]{1,0:T(8,128)(2,1)S(1)}, bf16[1024,256]{1,0:T(8,128)(2,1)S(1)}, bf16[8,144,256]{2,1,0:T(8,128)(2,1)S(1)}, bf16[8,144,256]{2,1,0:T(8,128)(2,1)S(1)}) custom-call(bf16[1088,768]{1,0:T(8,128)(2,1)S(1)} %get-tuple-element.29.x_wide, f32[1024,256]{1,0:T(8,128)S(1)} %get-tuple-element.30.preact_ref, ...), custom_call_target="tpu_custom_call" | custom-call | flops 1207959552 | bytes 1048576 | tf_op jit(solution)/shard_map/conv/pallas_call | solution.py:210
  13.2 5.0 %collective-permute-start.2 = (bf16[8,144,256]{2,1,0:T(8,128)(2,1)S(1)}, bf16[8,144,256]{2,1,0:T(8,128)(2,1)S(1)}, u32[]{:S(2)}, u32[]{:S(2)}) collective-permute-start(bf16[8,144,256]{2,1,0:T(8,128)(2,1)S(1)} %get-tuple-element.39), channel_id=1, source_target_pairs={{0,1},{1,0},{2,3},{3,2},{4,5},{5,4},{6,7},{7,6},{8,9},{9,8},{10,11... | collective-permute-start | bytes 1769480 | tf_op jit(solution)/shard_map/ppermute | solution.py:408
  18.2 1.6 %collective-permute-done.2 = bf16[8,144,256]{2,1,0:T(8,128)(2,1)S(1)} collective-permute-done((bf16[8,144,256]{2,1,0:T(8,128)(2,1)S(1)}, bf16[8,144,256]{2,1,0:T(8,128)(2,1)S(1)}, u32[]{:S(2)}, u32[]{:S(2)}) %collective-permute-start.2) | collective-permute-done | bytes 589856 | tf_op jit(solution)/shard_map/ppermute | solution.py:408
  19.9 0.0 copy-start
  19.9 0.0 copy-start.1
  19.9 0.1 add.3
  20.0 21.8 %all_to_all.20.wgrad_ref = bf16[8,144,256]{2,1,0:T(8,128)(2,1)S(1)} all-to-all(bf16[8,144,256]{2,1,0:T(8,128)(2,1)S(1)} %add.3), channel_id=1, replica_groups={{0,8,4,12,2,10,6,14},{1,9,5,13,3,11,7,15},{16,24,20,28,18,26,22,30},{17..., dimensions={0} | all-to-all | bytes 1179648 | tf_op jit(solution)/shard_map/all_to_all | solution.py:409
  41.8 0.0 copy-done
  41.8 0.0 copy-done.1
  41.8 0.2 matrix.1
  42.1 18.6 %all_to_all.21.p_ref = bf16[32,8,144]{2,1,0:T(8,128)(2,1)S(1)} all-to-all(bf16[32,8,144]{2,1,0:T(8,128)(2,1)S(1)} %broadcast_in_dim.8), channel_id=1, replica_groups=mesh['dp'=32,'tile'=16] {'dp'}, dimensions={0} | all-to-all | bytes 147456 | tf_op jit(solution)/shard_map/all_to_all | solution.py:372
  60.7 0.2 moment.1
  61.0 14.5 %all_to_all.22 = bf16[16,8,384]{2,1,0:T(8,128)(2,1)S(1)} all-to-all(bf16[16,8,384]{2,1,0:T(8,128)(2,1)S(1)} %broadcast_in_dim.9), channel_id=1, replica_groups=mesh['dp'=32,'tile'=16] {'tile'}, dimensions={0} | all-to-all | bytes 196608 | tf_op jit(solution)/shard_map/all_to_all | solution.py:372
  75.5 0.7 broadcast_in_dim.10
  76.1 3.9 %all-to-all-start.3 = ((bf16[32,8,256]{2,1,0:T(8,128)(2,1)}), bf16[32,8,256]{2,1,0:T(8,128)(2,1)S(1)}, u32[]{:S(2)}, u32[]{:S(2)}) async-start(bf16[32,8,256]{2,1,0:T(8,128)(2,1)} %broadcast_in_dim.10), calls=%async_computation.3 | async-start | bytes 262144 | tf_op jit(solution)/shard_map/all_to_all | solution.py:372
  80.0 3.1 %input_grad.1 = (bf16[1024,256]{1,0:T(8,128)(2,1)}, bf16[1024,256]{1,0:T(8,128)(2,1)}) custom-call(bf16[1024,256]{1,0:T(8,128)(2,1)S(1)} %get-tuple-element.34.out_ref, bf16[1024,256]{1,0:T(8,128)(2,1)S(1)} %get-tuple-element.35.slope_ref, bf16[2304,256]{1,0:T(8,128)(2,1)S(1)} %get-tuple-element.28.w_ref, ...), custom_call_target="tpu_custom_call" | custom-call | flops 1207959552 | bytes 2097152 | tf_op jit(solution)/shard_map/input_grad/pallas_call | solution.py:392
  83.1 1.4 %factor.1 = (f32[8,144]{1,0:T(8,128)}, f32[144,8]{1,0:T(8,128)S(1)}, f32[8,128]{1,0:T(8,128)S(1)}) custom-call(f32[8,128]{1,0:T(8,128)S(1)} %slice.9.gram_ref, f32[8,144]{1,0:T(8,128)S(1)} %get-tuple-element.43.p_ref), custom_call_target="tpu_custom_call" | custom-call | tf_op jit(solution)/shard_map/factor/pallas_call | solution.py:430
  84.5 4.9 %all-to-all-done.3.s_ref = bf16[32,8,256]{2,1,0:T(8,128)(2,1)S(1)} async-done(((bf16[32,8,256]{2,1,0:T(8,128)(2,1)}), bf16[32,8,256]{2,1,0:T(8,128)(2,1)S(1)}, u32[]{:S(2)}, u32[]{:S(2)}) %all-to-all-start.3) | async-done | bytes 131104 | tf_op jit(solution)/shard_map/all_to_all | solution.py:372
  89.4 0.9 %residual.1 = (f32[144,256]{1,0:T(8,128)}, f32[8,256]{1,0:T(8,128)}) custom-call(f32[144,256]{1,0:T(8,128)S(1)} %get-tuple-element.40.matrix_ref, f32[144,8]{1,0:T(8,128)S(1)} %get-tuple-element.45.columns_ref, f32[8,128]{1,0:T(8,128)S(1)} %get-tuple-element.46.solve_ref, bf16[32,8,256]{2,1,0:T(8,128)(2,1)S(1)} %all-to-all-done.3.s_ref), custom_call_target="tpu_custom_call" | custom-call | tf_op jit(solution)/shard_map/residual/pallas_call | solution.py:442
  (5 shorter events, 0.1 us)
Async XLA Ops:
  2.3 8.8 %collective-permute-start = (bf16[3,32,256]{2,1,0:T(8,128)(2,1)S(1)}, bf16[3,32,256]{2,1,0:T(8,128)(2,1)S(1)}, u32[]{:S(2)}, u32[]{:S(2)}) collective-permute-start(bf16[3,32,256]{2,1,0:T(8,128)(2,1)S(1)} %get-tuple-element.32.east_ref), channel_id=1, source_target_pairs={{0,1},{1,2},{2,3},{3,4},{4,5},{5,6},{6,7},{7,8},{8,9},{9,10},{10,1... | collective-permute-start | bytes 147464 | tf_op jit(solution)/shard_map/ppermute | solution.py:196
  5.8 5.3 %collective-permute-start.1 = (bf16[3,32,256]{2,1,0:T(8,128)(2,1)S(1)}, bf16[3,32,256]{2,1,0:T(8,128)(2,1)S(1)}, u32[]{:S(2)}, u32[]{:S(2)}) collective-permute-start(bf16[3,32,256]{2,1,0:T(8,128)(2,1)S(1)} %get-tuple-element.33.west_ref), channel_id=1, source_target_pairs={{0,15},{1,0},{2,1},{3,2},{4,3},{5,4},{6,5},{7,6},{8,7},{9,8},{10,9... | collective-permute-start | bytes 147464 | tf_op jit(solution)/shard_map/ppermute | solution.py:197
  13.2 6.6 %collective-permute-start.2 = (bf16[8,144,256]{2,1,0:T(8,128)(2,1)S(1)}, bf16[8,144,256]{2,1,0:T(8,128)(2,1)S(1)}, u32[]{:S(2)}, u32[]{:S(2)}) collective-permute-start(bf16[8,144,256]{2,1,0:T(8,128)(2,1)S(1)} %get-tuple-element.39), channel_id=1, source_target_pairs={{0,1},{1,0},{2,3},{3,2},{4,5},{5,4},{6,7},{7,6},{8,9},{9,8},{10,11... | collective-permute-start | bytes 1769480 | tf_op jit(solution)/shard_map/ppermute | solution.py:408
  19.9 21.9 %copy-start = (f32[1,144,256]{2,1,0:T(8,128)S(1)}, f32[1,144,256]{2,1,0:T(8,128)}, u32[]{:S(2)}) copy-start(f32[1,144,256]{2,1,0:T(8,128)} %param.8) | copy-start | bytes 442372
  19.9 21.9 %copy-start.1 = (f32[256,8]{0,1:T(8,128)S(1)}, f32[256,8]{0,1:T(8,128)}, u32[]{:S(2)}) copy-start(f32[256,8]{0,1:T(8,128)} %param.9) | copy-start | bytes 24580
  76.1 13.2 %all-to-all-start.3 = ((bf16[32,8,256]{2,1,0:T(8,128)(2,1)}), bf16[32,8,256]{2,1,0:T(8,128)(2,1)S(1)}, u32[]{:S(2)}, u32[]{:S(2)}) async-start(bf16[32,8,256]{2,1,0:T(8,128)(2,1)} %broadcast_in_dim.10), calls=%async_computation.3 | async-start | bytes 262144 | tf_op jit(solution)/shard_map/all_to_all | solution.py:372

commit v7 on v6

--- a/solution.py
+++ b/solution.py
@@ -370,7 +370,12 @@
 def shares_of(value, axis):
     count = lax.axis_size(axis)
     return lax.all_to_all(
-        jnp.broadcast_to(value[None], (count,) + value.shape), axis, 0, 0, tiled=True
+        jnp.broadcast_to(value[None], (count,) + value.shape),
+        axis,
+        0,
+        0,
+        axis_index_groups=[ring_order(count)],
+        tiled=True,
     )
 
 

time: 90.6 us -> 89.2 us (0.985)
  no operation moved by 1% of the time
where the time goes in v7:
time: 89.2 us; the launch traced here: 88.9 us
  blocking collectives  54.1 us (61%)
  starting transfers between devices  15.8 us (18%)
  Pallas kernels  11.5 us (13%)
  waiting for transfers between devices  5.91 us (7%)
    all_to_all x2, blocking collectives, shares_of(): lax.all_to_all(jnp.broadcast_to(value[None], (count,) + value.shape), axi...  32.3 us
    all_to_all x1, blocking collectives, per_device(): lax.all_to_all(summed, 'tile', 0, 0, axis_index_groups=chips('tile'), til...  21.8 us
    ppermute x1, starting transfers between devices, per_device(): summed = keep + lax.ppermute(send, 'tile', cores('tile'))  5.01 us
    all_to_all x1, waiting for transfers between devices, shares_of(): lax.all_to_all(jnp.broadcast_to(value[None], (count,) + value.shape), axi...  4.3 us
    all_to_all x1, starting transfers between devices, shares_of(): lax.all_to_all(jnp.broadcast_to(value[None], (count,) + value.shape), axi...  3.86 us
    ppermute x1, starting transfers between devices, conv_call(): left = lax.ppermute(east, 'tile', shift('tile', 1))  3.49 us
    ppermute x1, starting transfers between devices, conv_call(): right = lax.ppermute(west, 'tile', shift('tile', -1))  3.42 us
    pallas_call x1, Pallas kernels, per_device(): pl.pallas_call(functools.partial(input_grad_kernel, lat, lon), out_shape=...  3.09 us
  transfers between devices with their start and end apart: 4, of which 2 were waited for; matrix products, arithmetic and copies ran while one was open for 0% of the time, Pallas kernels for 7%

profile of v7, /device:TPU:1, one launch (start us, length us, event | category | flops | bytes accessed | tf_op | source)
XLA Modules:
  0.0 88.9 jit_solution(9500484661793449264)
XLA Ops:
  0.6 1.6 %load.1 = (bf16[1024,256]{1,0:T(8,128)(2,1)S(1)}, bf16[1024,256]{1,0:T(8,128)(2,1)S(1)}, bf16[2304,256]{1,0:T(8,128)(2,1)S(1)}, bf16[3,32,256]{2,1,0:T(8,128)(2,1)S(1)}, bf16[3,32,256]{2,1,0:T(8,128)(2,1)S(1)}) custom-call(bf16[1024,256]{1,0:T(8,128)(2,1)} %bitcast.11, bf16[1024,256]{1,0:T(8,128)(2,1)} %bitcast.12, bf16[2304,256]{1,0:T(8,128)(2,1)} %w_hbm.1), custom_call_target="tpu_custom_call" | custom-call | tf_op jit(solution)/shard_map/load/pallas_call | solution.py:187
  2.3 3.5 %collective-permute-start = (bf16[3,32,256]{2,1,0:T(8,128)(2,1)S(1)}, bf16[3,32,256]{2,1,0:T(8,128)(2,1)S(1)}, u32[]{:S(2)}, u32[]{:S(2)}) collective-permute-start(bf16[3,32,256]{2,1,0:T(8,128)(2,1)S(1)} %get-tuple-element.32.east_ref), channel_id=1, source_target_pairs={{0,1},{1,2},{2,3},{3,4},{4,5},{5,6},{6,7},{7,8},{8,9},{9,10},{10,1... | collective-permute-start | bytes 147464 | tf_op jit(solution)/shard_map/ppermute | solution.py:196
  5.8 3.4 %collective-permute-start.1 = (bf16[3,32,256]{2,1,0:T(8,128)(2,1)S(1)}, bf16[3,32,256]{2,1,0:T(8,128)(2,1)S(1)}, u32[]{:S(2)}, u32[]{:S(2)}) collective-permute-start(bf16[3,32,256]{2,1,0:T(8,128)(2,1)S(1)} %get-tuple-element.33.west_ref), channel_id=1, source_target_pairs={{0,15},{1,0},{2,1},{3,2},{4,3},{5,4},{6,5},{7,6},{8,7},{9,8},{10,9... | collective-permute-start | bytes 147464 | tf_op jit(solution)/shard_map/ppermute | solution.py:197
  9.2 1.8 %inner.1 = (bf16[1088,768]{1,0:T(8,128)(2,1)S(1)}, f32[1024,256]{1,0:T(8,128)S(1)}) custom-call(bf16[1024,256]{1,0:T(8,128)(2,1)S(1)} %get-tuple-element.27.x_ref, bf16[2304,256]{1,0:T(8,128)(2,1)S(1)} %get-tuple-element.28.w_ref), custom_call_target="tpu_custom_call" | custom-call | flops 1207959552 | tf_op jit(solution)/shard_map/inner/pallas_call | solution.py:198
  11.0 0.0 collective-permute-done.left_ref
  11.0 0.0 collective-permute-done.1.right_ref
  11.0 2.2 %conv.1 = (bf16[1024,256]{1,0:T(8,128)(2,1)S(1)}, bf16[1024,256]{1,0:T(8,128)(2,1)S(1)}, bf16[8,144,256]{2,1,0:T(8,128)(2,1)S(1)}, bf16[8,144,256]{2,1,0:T(8,128)(2,1)S(1)}) custom-call(bf16[1088,768]{1,0:T(8,128)(2,1)S(1)} %get-tuple-element.29.x_wide, f32[1024,256]{1,0:T(8,128)S(1)} %get-tuple-element.30.preact_ref, ...), custom_call_target="tpu_custom_call" | custom-call | flops 1207959552 | bytes 1048576 | tf_op jit(solution)/shard_map/conv/pallas_call | solution.py:210
  13.2 5.0 %collective-permute-start.2 = (bf16[8,144,256]{2,1,0:T(8,128)(2,1)S(1)}, bf16[8,144,256]{2,1,0:T(8,128)(2,1)S(1)}, u32[]{:S(2)}, u32[]{:S(2)}) collective-permute-start(bf16[8,144,256]{2,1,0:T(8,128)(2,1)S(1)} %get-tuple-element.39), channel_id=1, source_target_pairs={{0,1},{1,0},{2,3},{3,2},{4,5},{5,4},{6,7},{7,6},{8,9},{9,8},{10,11... | collective-permute-start | bytes 1769480 | tf_op jit(solution)/shard_map/ppermute | solution.py:413
  18.2 1.6 %collective-permute-done.2 = bf16[8,144,256]{2,1,0:T(8,128)(2,1)S(1)} collective-permute-done((bf16[8,144,256]{2,1,0:T(8,128)(2,1)S(1)}, bf16[8,144,256]{2,1,0:T(8,128)(2,1)S(1)}, u32[]{:S(2)}, u32[]{:S(2)}) %collective-permute-start.2) | collective-permute-done | bytes 589856 | tf_op jit(solution)/shard_map/ppermute | solution.py:413
  19.9 0.0 copy-start
  19.9 0.0 copy-start.1
  19.9 0.1 add.3
  20.0 21.8 %all_to_all.20.wgrad_ref = bf16[8,144,256]{2,1,0:T(8,128)(2,1)S(1)} all-to-all(bf16[8,144,256]{2,1,0:T(8,128)(2,1)S(1)} %add.3), channel_id=1, replica_groups={{0,8,4,12,2,10,6,14},{1,9,5,13,3,11,7,15},{16,24,20,28,18,26,22,30},{17..., dimensions={0} | all-to-all | bytes 1179648 | tf_op jit(solution)/shard_map/all_to_all | solution.py:414
  41.8 0.0 copy-done
  41.8 0.0 copy-done.1
  41.8 0.2 matrix.1
  42.1 18.2 %all_to_all.21.p_ref = bf16[32,8,144]{2,1,0:T(8,128)(2,1)S(1)} all-to-all(bf16[32,8,144]{2,1,0:T(8,128)(2,1)S(1)} %broadcast_in_dim.8), channel_id=1, replica_groups={{0,256,128,384,64,320,192,448,32,288,160,416,96,352,224,480,16,272,144,..., dimensions={0} | all-to-all | bytes 147456 | tf_op jit(solution)/shard_map/all_to_all | solution.py:372
  60.3 0.2 moment.1
  60.6 14.1 %all_to_all.22 = bf16[16,8,384]{2,1,0:T(8,128)(2,1)S(1)} all-to-all(bf16[16,8,384]{2,1,0:T(8,128)(2,1)S(1)} %broadcast_in_dim.9), channel_id=1, replica_groups={{0,8,4,12,2,10,6,14,1,9,5,13,3,11,7,15},{16,24,20,28,18,26,22,30,17,25,..., dimensions={0} | all-to-all | bytes 196608 | tf_op jit(solution)/shard_map/all_to_all | solution.py:372
  74.7 0.7 broadcast_in_dim.10
  75.3 3.9 %all-to-all-start.3 = ((bf16[32,8,256]{2,1,0:T(8,128)(2,1)}), bf16[32,8,256]{2,1,0:T(8,128)(2,1)S(1)}, u32[]{:S(2)}, u32[]{:S(2)}) async-start(bf16[32,8,256]{2,1,0:T(8,128)(2,1)} %broadcast_in_dim.10), calls=%async_computation.3 | async-start | bytes 262144 | tf_op jit(solution)/shard_map/all_to_all | solution.py:372
  79.2 3.1 %input_grad.1 = (bf16[1024,256]{1,0:T(8,128)(2,1)}, bf16[1024,256]{1,0:T(8,128)(2,1)}) custom-call(bf16[1024,256]{1,0:T(8,128)(2,1)S(1)} %get-tuple-element.34.out_ref, bf16[1024,256]{1,0:T(8,128)(2,1)S(1)} %get-tuple-element.35.slope_ref, bf16[2304,256]{1,0:T(8,128)(2,1)S(1)} %get-tuple-element.28.w_ref, ...), custom_call_target="tpu_custom_call" | custom-call | flops 1207959552 | bytes 2097152 | tf_op jit(solution)/shard_map/input_grad/pallas_call | solution.py:397
  82.3 1.4 %factor.1 = (f32[8,144]{1,0:T(8,128)}, f32[144,8]{1,0:T(8,128)S(1)}, f32[8,128]{1,0:T(8,128)S(1)}) custom-call(f32[8,128]{1,0:T(8,128)S(1)} %slice.9.gram_ref, f32[8,144]{1,0:T(8,128)S(1)} %get-tuple-element.43.p_ref), custom_call_target="tpu_custom_call" | custom-call | tf_op jit(solution)/shard_map/factor/pallas_call | solution.py:435
  83.7 4.3 %all-to-all-done.3.s_ref = bf16[32,8,256]{2,1,0:T(8,128)(2,1)S(1)} async-done(((bf16[32,8,256]{2,1,0:T(8,128)(2,1)}), bf16[32,8,256]{2,1,0:T(8,128)(2,1)S(1)}, u32[]{:S(2)}, u32[]{:S(2)}) %all-to-all-start.3) | async-done | bytes 131104 | tf_op jit(solution)/shard_map/all_to_all | solution.py:372
  88.0 0.9 %residual.1 = (f32[144,256]{1,0:T(8,128)}, f32[8,256]{1,0:T(8,128)}) custom-call(f32[144,256]{1,0:T(8,128)S(1)} %get-tuple-element.40.matrix_ref, f32[144,8]{1,0:T(8,128)S(1)} %get-tuple-element.45.columns_ref, f32[8,128]{1,0:T(8,128)S(1)} %get-tuple-element.46.solve_ref, bf16[32,8,256]{2,1,0:T(8,128)(2,1)S(1)} %all-to-all-done.3.s_ref), custom_call_target="tpu_custom_call" | custom-call | tf_op jit(solution)/shard_map/residual/pallas_call | solution.py:447
  (5 shorter events, 0.1 us)
Async XLA Ops:
  2.3 8.8 %collective-permute-start = (bf16[3,32,256]{2,1,0:T(8,128)(2,1)S(1)}, bf16[3,32,256]{2,1,0:T(8,128)(2,1)S(1)}, u32[]{:S(2)}, u32[]{:S(2)}) collective-permute-start(bf16[3,32,256]{2,1,0:T(8,128)(2,1)S(1)} %get-tuple-element.32.east_ref), channel_id=1, source_target_pairs={{0,1},{1,2},{2,3},{3,4},{4,5},{5,6},{6,7},{7,8},{8,9},{9,10},{10,1... | collective-permute-start | bytes 147464 | tf_op jit(solution)/shard_map/ppermute | solution.py:196
  5.8 5.3 %collective-permute-start.1 = (bf16[3,32,256]{2,1,0:T(8,128)(2,1)S(1)}, bf16[3,32,256]{2,1,0:T(8,128)(2,1)S(1)}, u32[]{:S(2)}, u32[]{:S(2)}) collective-permute-start(bf16[3,32,256]{2,1,0:T(8,128)(2,1)S(1)} %get-tuple-element.33.west_ref), channel_id=1, source_target_pairs={{0,15},{1,0},{2,1},{3,2},{4,3},{5,4},{6,5},{7,6},{8,7},{9,8},{10,9... | collective-permute-start | bytes 147464 | tf_op jit(solution)/shard_map/ppermute | solution.py:197
  13.2 6.6 %collective-permute-start.2 = (bf16[8,144,256]{2,1,0:T(8,128)(2,1)S(1)}, bf16[8,144,256]{2,1,0:T(8,128)(2,1)S(1)}, u32[]{:S(2)}, u32[]{:S(2)}) collective-permute-start(bf16[8,144,256]{2,1,0:T(8,128)(2,1)S(1)} %get-tuple-element.39), channel_id=1, source_target_pairs={{0,1},{1,0},{2,3},{3,2},{4,5},{5,4},{6,7},{7,6},{8,9},{9,8},{10,11... | collective-permute-start | bytes 1769480 | tf_op jit(solution)/shard_map/ppermute | solution.py:413
  19.9 21.9 %copy-start = (f32[1,144,256]{2,1,0:T(8,128)S(1)}, f32[1,144,256]{2,1,0:T(8,128)}, u32[]{:S(2)}) copy-start(f32[1,144,256]{2,1,0:T(8,128)} %param.8) | copy-start | bytes 442372
  19.9 21.9 %copy-start.1 = (f32[256,8]{0,1:T(8,128)S(1)}, f32[256,8]{0,1:T(8,128)}, u32[]{:S(2)}) copy-start(f32[256,8]{0,1:T(8,128)} %param.9) | copy-start | bytes 24580
  75.3 12.7 %all-to-all-start.3 = ((bf16[32,8,256]{2,1,0:T(8,128)(2,1)}), bf16[32,8,256]{2,1,0:T(8,128)(2,1)S(1)}, u32[]{:S(2)}, u32[]{:S(2)}) async-start(bf16[32,8,256]{2,1,0:T(8,128)(2,1)} %broadcast_in_dim.10), calls=%async_computation.3 | async-start | bytes 262144 | tf_op jit(solution)/shard_map/all_to_all | solution.py:372
